TPU v7x, 512 devices: a whole 4x8x8 slice. The times are simulated.
512 devices in a mesh: ctx: 128 (over y, z, core), tp: 4 (over x).
Axes of the slice: x: 4, y: 8, z: 8, core: 2. Of those that a mesh axis runs over, the one named last changes fastest.
Arguments:
- queries: bfloat16 [32768, 3072], P('ctx', 'tp'), may hold values from -24 to 24
- keys: bfloat16 [32768, 1024], P('ctx', 'tp'), may hold values from -6 to 6
- values: bfloat16 [32768, 1024], P('ctx', 'tp'), may hold values from -6 to 6
- doc_lengths: int32 [16], replicated, may hold values from 1 to 8192, 32768 in all
Outputs:
- attended: bfloat16 [32768, 3072], P(('ctx', 'tp'))
- log_total: float32 [24, 32768], P('tp', 'ctx')
Inputs may be any that keep to these rules, and one draw needn't show every extreme that they name: `doc_lengths`: the lengths sum to 32768; one of them is exactly 8192.
All inputs are finite; a program needn't handle non-finite values.
Results may differ from a plain program's by a relative error of at most 0.0054.
Values may be sent and summed in bfloat16 or wider, within the bound.
A program may use at most 64 MiB of HBM per device.

v0:
```python
import math

import jax
import jax.numpy as jnp
from jax import lax
from jax.sharding import PartitionSpec as P

HEAD_DIM = 128


NEG_FILL = -1e30


def shifted(block, axis, distance):
    devices = range(lax.axis_size(axis))
    route = [(i - distance, i) for i in devices if i - distance in devices]
    return lax.ppermute(block, axis, route)


def document_of(positions, doc_ends):
    return jnp.sum((positions[:, None] >= doc_ends[None, :]).astype(jnp.int32), axis=1)


def attend_block(
    carried, queries_local, query_pos, query_doc, key_block, value_block, key_pos, doc_ends
):
    key_doc = document_of(key_pos, doc_ends)
    allowed = (
        (query_doc[:, None] == key_doc[None, :])
        & (key_pos[None, :] <= query_pos[:, None])
        & (key_pos[None, :] >= 0)
    )
    key_heads = key_block.reshape(key_block.shape[0], -1, HEAD_DIM)
    value_heads = value_block.reshape(value_block.shape[0], -1, HEAD_DIM)
    score_scale = 1.0 / math.sqrt(HEAD_DIM)
    running_max, totals, accumulated = carried
    scores = (
        jnp.einsum("qhgd,khd->hgqk", queries_local, key_heads, preferred_element_type=jnp.float32)
        * score_scale
    )
    mask_full = allowed[None, None]
    new_max = jnp.maximum(running_max, jnp.max(jnp.where(mask_full, scores, NEG_FILL), axis=-1))
    weights = jnp.where(mask_full, jnp.exp(scores - new_max[..., None]), 0.0)
    factor = jnp.exp(running_max - new_max)
    totals = totals * factor + jnp.sum(weights, axis=-1)
    update = jnp.einsum(
        "hgqk,khd->qhgd",
        weights.astype(jnp.bfloat16),
        value_heads,
        preferred_element_type=jnp.float32,
    )
    accumulated = accumulated * jnp.transpose(factor, (2, 0, 1))[..., None] + update
    return (new_max, totals, accumulated)


def on_device(queries, keys, values, doc_lengths):
    row_count = queries.shape[0]
    rank_count = lax.axis_size("ctx")
    my_rank = lax.axis_index("ctx")
    reach_count = rank_count // 4
    kv_local = keys.shape[1] // HEAD_DIM
    group_size = queries.shape[1] // keys.shape[1]
    key_width = keys.shape[1]
    queries_local = queries.reshape(row_count, kv_local, group_size, HEAD_DIM)
    doc_ends = jnp.cumsum(doc_lengths)
    row_offsets = jnp.arange(row_count, dtype=jnp.int32)
    query_pos = my_rank * row_count + row_offsets
    query_doc = document_of(query_pos, doc_ends)
    stacked = jnp.concatenate([keys, values], axis=1)

    def attend_from(state, kv_block, source_rank):
        return attend_block(
            state,
            queries_local,
            query_pos,
            query_doc,
            kv_block[:, :key_width],
            kv_block[:, key_width:],
            source_rank * row_count + row_offsets,
            doc_ends,
        )

    initial = (
        jnp.full((kv_local, group_size, row_count), NEG_FILL, jnp.float32),
        jnp.zeros((kv_local, group_size, row_count), jnp.float32),
        jnp.zeros((row_count, kv_local, group_size, HEAD_DIM), jnp.float32),
    )
    state = attend_from(initial, stacked, my_rank)

    def cycle_step(step_index, loop_carry):
        moving, state_in = loop_carry
        moving = shifted(moving, "ctx", 1)
        return (moving, attend_from(state_in, moving, my_rank - step_index))

    state = lax.fori_loop(1, reach_count + 1, cycle_step, (stacked, state))[1]
    running_max, totals, accumulated = state
    attended = (
        (accumulated / jnp.transpose(totals, (2, 0, 1))[..., None])
        .astype(jnp.bfloat16)
        .reshape(row_count, -1)
    )
    log_total = (running_max + jnp.log(totals)).reshape(-1, row_count)
    token_major = lax.all_to_all(attended, "tp", split_axis=0, concat_axis=1, tiled=True)
    return (token_major, log_total)


def solution(mesh):
    in_specs = (P("ctx", "tp"), P("ctx", "tp"), P("ctx", "tp"), P())
    out_specs = (P(("ctx", "tp"), None), P("tp", "ctx"))
    return jax.shard_map(
        on_device, mesh=mesh, in_specs=in_specs, out_specs=out_specs, check_vma=False
    )
```

profile of v0, /device:TPU:32, one launch (start us, length us, event | category | flops | bytes accessed | tf_op | source)
XLA Modules:
  0.0 431.5 jit_solution(12892544017025143577)
XLA Ops:
  8.5 408.9 %while.20 = (s32[]{:T(128)}, bf16[256,512]{0,1:T(8,128)(2,1)S(1)}, f32[2,3,256]{2,1,0:T(4,128)S(1)}, f32[2,3,256]{2,1,0:T(4,128)S(1)}, f32[256,2,3,128]{3,0,2,1:...) while((s32[]{:T(128)}, bf16[256,512]{0,1:T(8,128)(2,1)S(1)}, ...), condition=%wide.region_8.9_spmd.clone, body=%wide.region_4.0_spmd.clone.sunk | while | flops 205538560 | bytes 9413377 | solution.py:95
  8.5 1.9 collective-permute-start
  10.7 12.1 %collective-permute-done = bf16[256,512]{0,1:T(8,128)(2,1)S(1)} collective-permute-done((bf16[256,512]{0,1:T(8,128)(2,1)S(1)}, bf16[256,512]{0,1:T(8,128)(2,1)S(1)}, u32[]{:S(2)}, u32[]{:S(2)}) %collective-permute-start) | collective-permute-done | bytes 262176 | tf_op jit(solution)/shard_map/while/body/eval_jaxpr/ppermute | solution.py:17
  24.5 1.9 collective-permute-start
  26.7 8.8 %collective-permute-done = bf16[256,512]{0,1:T(8,128)(2,1)S(1)} collective-permute-done((bf16[256,512]{0,1:T(8,128)(2,1)S(1)}, bf16[256,512]{0,1:T(8,128)(2,1)S(1)}, u32[]{:S(2)}, u32[]{:S(2)}) %collective-permute-start) | collective-permute-done | bytes 262176 | tf_op jit(solution)/shard_map/while/body/eval_jaxpr/ppermute | solution.py:17
  37.2 1.9 collective-permute-start
  39.4 8.8 %collective-permute-done = bf16[256,512]{0,1:T(8,128)(2,1)S(1)} collective-permute-done((bf16[256,512]{0,1:T(8,128)(2,1)S(1)}, bf16[256,512]{0,1:T(8,128)(2,1)S(1)}, u32[]{:S(2)}, u32[]{:S(2)}) %collective-permute-start) | collective-permute-done | bytes 262176 | tf_op jit(solution)/shard_map/while/body/eval_jaxpr/ppermute | solution.py:17
  49.8 1.9 collective-permute-start
  52.1 8.8 %collective-permute-done = bf16[256,512]{0,1:T(8,128)(2,1)S(1)} collective-permute-done((bf16[256,512]{0,1:T(8,128)(2,1)S(1)}, bf16[256,512]{0,1:T(8,128)(2,1)S(1)}, u32[]{:S(2)}, u32[]{:S(2)}) %collective-permute-start) | collective-permute-done | bytes 262176 | tf_op jit(solution)/shard_map/while/body/eval_jaxpr/ppermute | solution.py:17
  62.5 1.9 collective-permute-start
  64.7 8.8 %collective-permute-done = bf16[256,512]{0,1:T(8,128)(2,1)S(1)} collective-permute-done((bf16[256,512]{0,1:T(8,128)(2,1)S(1)}, bf16[256,512]{0,1:T(8,128)(2,1)S(1)}, u32[]{:S(2)}, u32[]{:S(2)}) %collective-permute-start) | collective-permute-done | bytes 262176 | tf_op jit(solution)/shard_map/while/body/eval_jaxpr/ppermute | solution.py:17
  77.4 8.8 %collective-permute-done = bf16[256,512]{0,1:T(8,128)(2,1)S(1)} collective-permute-done((bf16[256,512]{0,1:T(8,128)(2,1)S(1)}, bf16[256,512]{0,1:T(8,128)(2,1)S(1)}, u32[]{:S(2)}, u32[]{:S(2)}) %collective-permute-start) | collective-permute-done | bytes 262176 | tf_op jit(solution)/shard_map/while/body/eval_jaxpr/ppermute | solution.py:17
  90.1 8.8 %collective-permute-done = bf16[256,512]{0,1:T(8,128)(2,1)S(1)} collective-permute-done((bf16[256,512]{0,1:T(8,128)(2,1)S(1)}, bf16[256,512]{0,1:T(8,128)(2,1)S(1)}, u32[]{:S(2)}, u32[]{:S(2)}) %collective-permute-start) | collective-permute-done | bytes 262176 | tf_op jit(solution)/shard_map/while/body/eval_jaxpr/ppermute | solution.py:17
  102.8 8.8 %collective-permute-done = bf16[256,512]{0,1:T(8,128)(2,1)S(1)} collective-permute-done((bf16[256,512]{0,1:T(8,128)(2,1)S(1)}, bf16[256,512]{0,1:T(8,128)(2,1)S(1)}, u32[]{:S(2)}, u32[]{:S(2)}) %collective-permute-start) | collective-permute-done | bytes 262176 | tf_op jit(solution)/shard_map/while/body/eval_jaxpr/ppermute | solution.py:17
  113.2 1.9 collective-permute-start
  115.4 8.8 %collective-permute-done = bf16[256,512]{0,1:T(8,128)(2,1)S(1)} collective-permute-done((bf16[256,512]{0,1:T(8,128)(2,1)S(1)}, bf16[256,512]{0,1:T(8,128)(2,1)S(1)}, u32[]{:S(2)}, u32[]{:S(2)}) %collective-permute-start) | collective-permute-done | bytes 262176 | tf_op jit(solution)/shard_map/while/body/eval_jaxpr/ppermute | solution.py:17
  128.1 8.8 %collective-permute-done = bf16[256,512]{0,1:T(8,128)(2,1)S(1)} collective-permute-done((bf16[256,512]{0,1:T(8,128)(2,1)S(1)}, bf16[256,512]{0,1:T(8,128)(2,1)S(1)}, u32[]{:S(2)}, u32[]{:S(2)}) %collective-permute-start) | collective-permute-done | bytes 262176 | tf_op jit(solution)/shard_map/while/body/eval_jaxpr/ppermute | solution.py:17
  140.8 8.8 %collective-permute-done = bf16[256,512]{0,1:T(8,128)(2,1)S(1)} collective-permute-done((bf16[256,512]{0,1:T(8,128)(2,1)S(1)}, bf16[256,512]{0,1:T(8,128)(2,1)S(1)}, u32[]{:S(2)}, u32[]{:S(2)}) %collective-permute-start) | collective-permute-done | bytes 262176 | tf_op jit(solution)/shard_map/while/body/eval_jaxpr/ppermute | solution.py:17
  153.4 8.8 %collective-permute-done = bf16[256,512]{0,1:T(8,128)(2,1)S(1)} collective-permute-done((bf16[256,512]{0,1:T(8,128)(2,1)S(1)}, bf16[256,512]{0,1:T(8,128)(2,1)S(1)}, u32[]{:S(2)}, u32[]{:S(2)}) %collective-permute-start) | collective-permute-done | bytes 262176 | tf_op jit(solution)/shard_map/while/body/eval_jaxpr/ppermute | solution.py:17
  163.9 1.9 collective-permute-start
  166.1 8.8 %collective-permute-done = bf16[256,512]{0,1:T(8,128)(2,1)S(1)} collective-permute-done((bf16[256,512]{0,1:T(8,128)(2,1)S(1)}, bf16[256,512]{0,1:T(8,128)(2,1)S(1)}, u32[]{:S(2)}, u32[]{:S(2)}) %collective-permute-start) | collective-permute-done | bytes 262176 | tf_op jit(solution)/shard_map/while/body/eval_jaxpr/ppermute | solution.py:17
  176.6 1.9 collective-permute-start
  178.8 8.8 %collective-permute-done = bf16[256,512]{0,1:T(8,128)(2,1)S(1)} collective-permute-done((bf16[256,512]{0,1:T(8,128)(2,1)S(1)}, bf16[256,512]{0,1:T(8,128)(2,1)S(1)}, u32[]{:S(2)}, u32[]{:S(2)}) %collective-permute-start) | collective-permute-done | bytes 262176 | tf_op jit(solution)/shard_map/while/body/eval_jaxpr/ppermute | solution.py:17
  191.5 8.8 %collective-permute-done = bf16[256,512]{0,1:T(8,128)(2,1)S(1)} collective-permute-done((bf16[256,512]{0,1:T(8,128)(2,1)S(1)}, bf16[256,512]{0,1:T(8,128)(2,1)S(1)}, u32[]{:S(2)}, u32[]{:S(2)}) %collective-permute-start) | collective-permute-done | bytes 262176 | tf_op jit(solution)/shard_map/while/body/eval_jaxpr/ppermute | solution.py:17
  204.1 8.8 %collective-permute-done = bf16[256,512]{0,1:T(8,128)(2,1)S(1)} collective-permute-done((bf16[256,512]{0,1:T(8,128)(2,1)S(1)}, bf16[256,512]{0,1:T(8,128)(2,1)S(1)}, u32[]{:S(2)}, u32[]{:S(2)}) %collective-permute-start) | collective-permute-done | bytes 262176 | tf_op jit(solution)/shard_map/while/body/eval_jaxpr/ppermute | solution.py:17
  216.8 8.8 %collective-permute-done = bf16[256,512]{0,1:T(8,128)(2,1)S(1)} collective-permute-done((bf16[256,512]{0,1:T(8,128)(2,1)S(1)}, bf16[256,512]{0,1:T(8,128)(2,1)S(1)}, u32[]{:S(2)}, u32[]{:S(2)}) %collective-permute-start) | collective-permute-done | bytes 262176 | tf_op jit(solution)/shard_map/while/body/eval_jaxpr/ppermute | solution.py:17
  227.3 1.9 collective-permute-start
  229.5 8.8 %collective-permute-done = bf16[256,512]{0,1:T(8,128)(2,1)S(1)} collective-permute-done((bf16[256,512]{0,1:T(8,128)(2,1)S(1)}, bf16[256,512]{0,1:T(8,128)(2,1)S(1)}, u32[]{:S(2)}, u32[]{:S(2)}) %collective-permute-start) | collective-permute-done | bytes 262176 | tf_op jit(solution)/shard_map/while/body/eval_jaxpr/ppermute | solution.py:17
  239.9 1.9 collective-permute-start
  242.2 8.8 %collective-permute-done = bf16[256,512]{0,1:T(8,128)(2,1)S(1)} collective-permute-done((bf16[256,512]{0,1:T(8,128)(2,1)S(1)}, bf16[256,512]{0,1:T(8,128)(2,1)S(1)}, u32[]{:S(2)}, u32[]{:S(2)}) %collective-permute-start) | collective-permute-done | bytes 262176 | tf_op jit(solution)/shard_map/while/body/eval_jaxpr/ppermute | solution.py:17
  254.8 8.8 %collective-permute-done = bf16[256,512]{0,1:T(8,128)(2,1)S(1)} collective-permute-done((bf16[256,512]{0,1:T(8,128)(2,1)S(1)}, bf16[256,512]{0,1:T(8,128)(2,1)S(1)}, u32[]{:S(2)}, u32[]{:S(2)}) %collective-permute-start) | collective-permute-done | bytes 262176 | tf_op jit(solution)/shard_map/while/body/eval_jaxpr/ppermute | solution.py:17
  267.5 8.8 %collective-permute-done = bf16[256,512]{0,1:T(8,128)(2,1)S(1)} collective-permute-done((bf16[256,512]{0,1:T(8,128)(2,1)S(1)}, bf16[256,512]{0,1:T(8,128)(2,1)S(1)}, u32[]{:S(2)}, u32[]{:S(2)}) %collective-permute-start) | collective-permute-done | bytes 262176 | tf_op jit(solution)/shard_map/while/body/eval_jaxpr/ppermute | solution.py:17
  280.2 8.8 %collective-permute-done = bf16[256,512]{0,1:T(8,128)(2,1)S(1)} collective-permute-done((bf16[256,512]{0,1:T(8,128)(2,1)S(1)}, bf16[256,512]{0,1:T(8,128)(2,1)S(1)}, u32[]{:S(2)}, u32[]{:S(2)}) %collective-permute-start) | collective-permute-done | bytes 262176 | tf_op jit(solution)/shard_map/while/body/eval_jaxpr/ppermute | solution.py:17
  290.6 1.9 collective-permute-start
  292.9 8.8 %collective-permute-done = bf16[256,512]{0,1:T(8,128)(2,1)S(1)} collective-permute-done((bf16[256,512]{0,1:T(8,128)(2,1)S(1)}, bf16[256,512]{0,1:T(8,128)(2,1)S(1)}, u32[]{:S(2)}, u32[]{:S(2)}) %collective-permute-start) | collective-permute-done | bytes 262176 | tf_op jit(solution)/shard_map/while/body/eval_jaxpr/ppermute | solution.py:17
  305.5 8.8 %collective-permute-done = bf16[256,512]{0,1:T(8,128)(2,1)S(1)} collective-permute-done((bf16[256,512]{0,1:T(8,128)(2,1)S(1)}, bf16[256,512]{0,1:T(8,128)(2,1)S(1)}, u32[]{:S(2)}, u32[]{:S(2)}) %collective-permute-start) | collective-permute-done | bytes 262176 | tf_op jit(solution)/shard_map/while/body/eval_jaxpr/ppermute | solution.py:17
  318.2 8.8 %collective-permute-done = bf16[256,512]{0,1:T(8,128)(2,1)S(1)} collective-permute-done((bf16[256,512]{0,1:T(8,128)(2,1)S(1)}, bf16[256,512]{0,1:T(8,128)(2,1)S(1)}, u32[]{:S(2)}, u32[]{:S(2)}) %collective-permute-start) | collective-permute-done | bytes 262176 | tf_op jit(solution)/shard_map/while/body/eval_jaxpr/ppermute | solution.py:17
  330.9 8.8 %collective-permute-done = bf16[256,512]{0,1:T(8,128)(2,1)S(1)} collective-permute-done((bf16[256,512]{0,1:T(8,128)(2,1)S(1)}, bf16[256,512]{0,1:T(8,128)(2,1)S(1)}, u32[]{:S(2)}, u32[]{:S(2)}) %collective-permute-start) | collective-permute-done | bytes 262176 | tf_op jit(solution)/shard_map/while/body/eval_jaxpr/ppermute | solution.py:17
  343.6 8.8 %collective-permute-done = bf16[256,512]{0,1:T(8,128)(2,1)S(1)} collective-permute-done((bf16[256,512]{0,1:T(8,128)(2,1)S(1)}, bf16[256,512]{0,1:T(8,128)(2,1)S(1)}, u32[]{:S(2)}, u32[]{:S(2)}) %collective-permute-start) | collective-permute-done | bytes 262176 | tf_op jit(solution)/shard_map/while/body/eval_jaxpr/ppermute | solution.py:17
  354.0 1.9 collective-permute-start
  356.2 8.8 %collective-permute-done = bf16[256,512]{0,1:T(8,128)(2,1)S(1)} collective-permute-done((bf16[256,512]{0,1:T(8,128)(2,1)S(1)}, bf16[256,512]{0,1:T(8,128)(2,1)S(1)}, u32[]{:S(2)}, u32[]{:S(2)}) %collective-permute-start) | collective-permute-done | bytes 262176 | tf_op jit(solution)/shard_map/while/body/eval_jaxpr/ppermute | solution.py:17
  368.9 8.8 %collective-permute-done = bf16[256,512]{0,1:T(8,128)(2,1)S(1)} collective-permute-done((bf16[256,512]{0,1:T(8,128)(2,1)S(1)}, bf16[256,512]{0,1:T(8,128)(2,1)S(1)}, u32[]{:S(2)}, u32[]{:S(2)}) %collective-permute-start) | collective-permute-done | bytes 262176 | tf_op jit(solution)/shard_map/while/body/eval_jaxpr/ppermute | solution.py:17
  381.6 8.8 %collective-permute-done = bf16[256,512]{0,1:T(8,128)(2,1)S(1)} collective-permute-done((bf16[256,512]{0,1:T(8,128)(2,1)S(1)}, bf16[256,512]{0,1:T(8,128)(2,1)S(1)}, u32[]{:S(2)}, u32[]{:S(2)}) %collective-permute-start) | collective-permute-done | bytes 262176 | tf_op jit(solution)/shard_map/while/body/eval_jaxpr/ppermute | solution.py:17
  394.2 8.8 %collective-permute-done = bf16[256,512]{0,1:T(8,128)(2,1)S(1)} collective-permute-done((bf16[256,512]{0,1:T(8,128)(2,1)S(1)}, bf16[256,512]{0,1:T(8,128)(2,1)S(1)}, u32[]{:S(2)}, u32[]{:S(2)}) %collective-permute-start) | collective-permute-done | bytes 262176 | tf_op jit(solution)/shard_map/while/body/eval_jaxpr/ppermute | solution.py:17
  404.7 1.9 collective-permute-start
  406.9 8.8 %collective-permute-done = bf16[256,512]{0,1:T(8,128)(2,1)S(1)} collective-permute-done((bf16[256,512]{0,1:T(8,128)(2,1)S(1)}, bf16[256,512]{0,1:T(8,128)(2,1)S(1)}, u32[]{:S(2)}, u32[]{:S(2)}) %collective-permute-start) | collective-permute-done | bytes 262176 | tf_op jit(solution)/shard_map/while/body/eval_jaxpr/ppermute | solution.py:17
  419.1 4.3 all-to-all-start
  424.0 6.8 %all-to-all-done = bf16[4,64,768]{2,1,0:T(8,128)(2,1)S(1)} async-done(((bf16[4,64,768]{2,1,0:T(8,128)(2,1)}), bf16[4,64,768]{2,1,0:T(8,128)(2,1)S(1)}, u32[]{:S(2)}, u32[]{:S(2)}) %all-to-all-start) | async-done | bytes 393248 | tf_op jit(solution)/shard_map/all_to_all | solution.py:103
  (428 shorter events, 107.3 us)
Async XLA Ops:
  8.5 14.3 %collective-permute-start = (bf16[256,512]{0,1:T(8,128)(2,1)S(1)}, bf16[256,512]{0,1:T(8,128)(2,1)S(1)}, u32[]{:S(2)}, u32[]{:S(2)}) collective-permute-start(bf16[256,512]{0,1:T(8,128)(2,1)S(1)} %get-tuple-element.367), channel_id=1, source_target_pairs={{0,4},{4,8},{8,12},{12,16},{16,20},{20,24},{24,28},{28,32},{32,36}... | collective-permute-start | bytes 786440 | tf_op jit(solution)/shard_map/while/body/eval_jaxpr/ppermute | solution.py:17
  24.5 11.0 %collective-permute-start = (bf16[256,512]{0,1:T(8,128)(2,1)S(1)}, bf16[256,512]{0,1:T(8,128)(2,1)S(1)}, u32[]{:S(2)}, u32[]{:S(2)}) collective-permute-start(bf16[256,512]{0,1:T(8,128)(2,1)S(1)} %get-tuple-element.367), channel_id=1, source_target_pairs={{0,4},{4,8},{8,12},{12,16},{16,20},{20,24},{24,28},{28,32},{32,36}... | collective-permute-start | bytes 786440 | tf_op jit(solution)/shard_map/while/body/eval_jaxpr/ppermute | solution.py:17
  37.2 11.0 %collective-permute-start = (bf16[256,512]{0,1:T(8,128)(2,1)S(1)}, bf16[256,512]{0,1:T(8,128)(2,1)S(1)}, u32[]{:S(2)}, u32[]{:S(2)}) collective-permute-start(bf16[256,512]{0,1:T(8,128)(2,1)S(1)} %get-tuple-element.367), channel_id=1, source_target_pairs={{0,4},{4,8},{8,12},{12,16},{16,20},{20,24},{24,28},{28,32},{32,36}... | collective-permute-start | bytes 786440 | tf_op jit(solution)/shard_map/while/body/eval_jaxpr/ppermute | solution.py:17
  49.8 11.0 %collective-permute-start = (bf16[256,512]{0,1:T(8,128)(2,1)S(1)}, bf16[256,512]{0,1:T(8,128)(2,1)S(1)}, u32[]{:S(2)}, u32[]{:S(2)}) collective-permute-start(bf16[256,512]{0,1:T(8,128)(2,1)S(1)} %get-tuple-element.367), channel_id=1, source_target_pairs={{0,4},{4,8},{8,12},{12,16},{16,20},{20,24},{24,28},{28,32},{32,36}... | collective-permute-start | bytes 786440 | tf_op jit(solution)/shard_map/while/body/eval_jaxpr/ppermute | solution.py:17
  62.5 11.0 %collective-permute-start = (bf16[256,512]{0,1:T(8,128)(2,1)S(1)}, bf16[256,512]{0,1:T(8,128)(2,1)S(1)}, u32[]{:S(2)}, u32[]{:S(2)}) collective-permute-start(bf16[256,512]{0,1:T(8,128)(2,1)S(1)} %get-tuple-element.367), channel_id=1, source_target_pairs={{0,4},{4,8},{8,12},{12,16},{16,20},{20,24},{24,28},{28,32},{32,36}... | collective-permute-start | bytes 786440 | tf_op jit(solution)/shard_map/while/body/eval_jaxpr/ppermute | solution.py:17
  75.2 11.0 %collective-permute-start = (bf16[256,512]{0,1:T(8,128)(2,1)S(1)}, bf16[256,512]{0,1:T(8,128)(2,1)S(1)}, u32[]{:S(2)}, u32[]{:S(2)}) collective-permute-start(bf16[256,512]{0,1:T(8,128)(2,1)S(1)} %get-tuple-element.367), channel_id=1, source_target_pairs={{0,4},{4,8},{8,12},{12,16},{16,20},{20,24},{24,28},{28,32},{32,36}... | collective-permute-start | bytes 786440 | tf_op jit(solution)/shard_map/while/body/eval_jaxpr/ppermute | solution.py:17
  87.9 11.0 %collective-permute-start = (bf16[256,512]{0,1:T(8,128)(2,1)S(1)}, bf16[256,512]{0,1:T(8,128)(2,1)S(1)}, u32[]{:S(2)}, u32[]{:S(2)}) collective-permute-start(bf16[256,512]{0,1:T(8,128)(2,1)S(1)} %get-tuple-element.367), channel_id=1, source_target_pairs={{0,4},{4,8},{8,12},{12,16},{16,20},{20,24},{24,28},{28,32},{32,36}... | collective-permute-start | bytes 786440 | tf_op jit(solution)/shard_map/while/body/eval_jaxpr/ppermute | solution.py:17
  100.5 11.0 %collective-permute-start = (bf16[256,512]{0,1:T(8,128)(2,1)S(1)}, bf16[256,512]{0,1:T(8,128)(2,1)S(1)}, u32[]{:S(2)}, u32[]{:S(2)}) collective-permute-start(bf16[256,512]{0,1:T(8,128)(2,1)S(1)} %get-tuple-element.367), channel_id=1, source_target_pairs={{0,4},{4,8},{8,12},{12,16},{16,20},{20,24},{24,28},{28,32},{32,36}... | collective-permute-start | bytes 786440 | tf_op jit(solution)/shard_map/while/body/eval_jaxpr/ppermute | solution.py:17
  113.2 11.0 %collective-permute-start = (bf16[256,512]{0,1:T(8,128)(2,1)S(1)}, bf16[256,512]{0,1:T(8,128)(2,1)S(1)}, u32[]{:S(2)}, u32[]{:S(2)}) collective-permute-start(bf16[256,512]{0,1:T(8,128)(2,1)S(1)} %get-tuple-element.367), channel_id=1, source_target_pairs={{0,4},{4,8},{8,12},{12,16},{16,20},{20,24},{24,28},{28,32},{32,36}... | collective-permute-start | bytes 786440 | tf_op jit(solution)/shard_map/while/body/eval_jaxpr/ppermute | solution.py:17
  125.9 11.0 %collective-permute-start = (bf16[256,512]{0,1:T(8,128)(2,1)S(1)}, bf16[256,512]{0,1:T(8,128)(2,1)S(1)}, u32[]{:S(2)}, u32[]{:S(2)}) collective-permute-start(bf16[256,512]{0,1:T(8,128)(2,1)S(1)} %get-tuple-element.367), channel_id=1, source_target_pairs={{0,4},{4,8},{8,12},{12,16},{16,20},{20,24},{24,28},{28,32},{32,36}... | collective-permute-start | bytes 786440 | tf_op jit(solution)/shard_map/while/body/eval_jaxpr/ppermute | solution.py:17
  138.6 11.0 %collective-permute-start = (bf16[256,512]{0,1:T(8,128)(2,1)S(1)}, bf16[256,512]{0,1:T(8,128)(2,1)S(1)}, u32[]{:S(2)}, u32[]{:S(2)}) collective-permute-start(bf16[256,512]{0,1:T(8,128)(2,1)S(1)} %get-tuple-element.367), channel_id=1, source_target_pairs={{0,4},{4,8},{8,12},{12,16},{16,20},{20,24},{24,28},{28,32},{32,36}... | collective-permute-start | bytes 786440 | tf_op jit(solution)/shard_map/while/body/eval_jaxpr/ppermute | solution.py:17
  151.2 11.0 %collective-permute-start = (bf16[256,512]{0,1:T(8,128)(2,1)S(1)}, bf16[256,512]{0,1:T(8,128)(2,1)S(1)}, u32[]{:S(2)}, u32[]{:S(2)}) collective-permute-start(bf16[256,512]{0,1:T(8,128)(2,1)S(1)} %get-tuple-element.367), channel_id=1, source_target_pairs={{0,4},{4,8},{8,12},{12,16},{16,20},{20,24},{24,28},{28,32},{32,36}... | collective-permute-start | bytes 786440 | tf_op jit(solution)/shard_map/while/body/eval_jaxpr/ppermute | solution.py:17
  163.9 11.0 %collective-permute-start = (bf16[256,512]{0,1:T(8,128)(2,1)S(1)}, bf16[256,512]{0,1:T(8,128)(2,1)S(1)}, u32[]{:S(2)}, u32[]{:S(2)}) collective-permute-start(bf16[256,512]{0,1:T(8,128)(2,1)S(1)} %get-tuple-element.367), channel_id=1, source_target_pairs={{0,4},{4,8},{8,12},{12,16},{16,20},{20,24},{24,28},{28,32},{32,36}... | collective-permute-start | bytes 786440 | tf_op jit(solution)/shard_map/while/body/eval_jaxpr/ppermute | solution.py:17
  176.6 11.0 %collective-permute-start = (bf16[256,512]{0,1:T(8,128)(2,1)S(1)}, bf16[256,512]{0,1:T(8,128)(2,1)S(1)}, u32[]{:S(2)}, u32[]{:S(2)}) collective-permute-start(bf16[256,512]{0,1:T(8,128)(2,1)S(1)} %get-tuple-element.367), channel_id=1, source_target_pairs={{0,4},{4,8},{8,12},{12,16},{16,20},{20,24},{24,28},{28,32},{32,36}... | collective-permute-start | bytes 786440 | tf_op jit(solution)/shard_map/while/body/eval_jaxpr/ppermute | solution.py:17
  189.2 11.0 %collective-permute-start = (bf16[256,512]{0,1:T(8,128)(2,1)S(1)}, bf16[256,512]{0,1:T(8,128)(2,1)S(1)}, u32[]{:S(2)}, u32[]{:S(2)}) collective-permute-start(bf16[256,512]{0,1:T(8,128)(2,1)S(1)} %get-tuple-element.367), channel_id=1, source_target_pairs={{0,4},{4,8},{8,12},{12,16},{16,20},{20,24},{24,28},{28,32},{32,36}... | collective-permute-start | bytes 786440 | tf_op jit(solution)/shard_map/while/body/eval_jaxpr/ppermute | solution.py:17
  201.9 11.0 %collective-permute-start = (bf16[256,512]{0,1:T(8,128)(2,1)S(1)}, bf16[256,512]{0,1:T(8,128)(2,1)S(1)}, u32[]{:S(2)}, u32[]{:S(2)}) collective-permute-start(bf16[256,512]{0,1:T(8,128)(2,1)S(1)} %get-tuple-element.367), channel_id=1, source_target_pairs={{0,4},{4,8},{8,12},{12,16},{16,20},{20,24},{24,28},{28,32},{32,36}... | collective-permute-start | bytes 786440 | tf_op jit(solution)/shard_map/while/body/eval_jaxpr/ppermute | solution.py:17
  214.6 11.0 %collective-permute-start = (bf16[256,512]{0,1:T(8,128)(2,1)S(1)}, bf16[256,512]{0,1:T(8,128)(2,1)S(1)}, u32[]{:S(2)}, u32[]{:S(2)}) collective-permute-start(bf16[256,512]{0,1:T(8,128)(2,1)S(1)} %get-tuple-element.367), channel_id=1, source_target_pairs={{0,4},{4,8},{8,12},{12,16},{16,20},{20,24},{24,28},{28,32},{32,36}... | collective-permute-start | bytes 786440 | tf_op jit(solution)/shard_map/while/body/eval_jaxpr/ppermute | solution.py:17
  227.3 11.0 %collective-permute-start = (bf16[256,512]{0,1:T(8,128)(2,1)S(1)}, bf16[256,512]{0,1:T(8,128)(2,1)S(1)}, u32[]{:S(2)}, u32[]{:S(2)}) collective-permute-start(bf16[256,512]{0,1:T(8,128)(2,1)S(1)} %get-tuple-element.367), channel_id=1, source_target_pairs={{0,4},{4,8},{8,12},{12,16},{16,20},{20,24},{24,28},{28,32},{32,36}... | collective-permute-start | bytes 786440 | tf_op jit(solution)/shard_map/while/body/eval_jaxpr/ppermute | solution.py:17
  239.9 11.0 %collective-permute-start = (bf16[256,512]{0,1:T(8,128)(2,1)S(1)}, bf16[256,512]{0,1:T(8,128)(2,1)S(1)}, u32[]{:S(2)}, u32[]{:S(2)}) collective-permute-start(bf16[256,512]{0,1:T(8,128)(2,1)S(1)} %get-tuple-element.367), channel_id=1, source_target_pairs={{0,4},{4,8},{8,12},{12,16},{16,20},{20,24},{24,28},{28,32},{32,36}... | collective-permute-start | bytes 786440 | tf_op jit(solution)/shard_map/while/body/eval_jaxpr/ppermute | solution.py:17
  252.6 11.0 %collective-permute-start = (bf16[256,512]{0,1:T(8,128)(2,1)S(1)}, bf16[256,512]{0,1:T(8,128)(2,1)S(1)}, u32[]{:S(2)}, u32[]{:S(2)}) collective-permute-start(bf16[256,512]{0,1:T(8,128)(2,1)S(1)} %get-tuple-element.367), channel_id=1, source_target_pairs={{0,4},{4,8},{8,12},{12,16},{16,20},{20,24},{24,28},{28,32},{32,36}... | collective-permute-start | bytes 786440 | tf_op jit(solution)/shard_map/while/body/eval_jaxpr/ppermute | solution.py:17
  265.3 11.0 %collective-permute-start = (bf16[256,512]{0,1:T(8,128)(2,1)S(1)}, bf16[256,512]{0,1:T(8,128)(2,1)S(1)}, u32[]{:S(2)}, u32[]{:S(2)}) collective-permute-start(bf16[256,512]{0,1:T(8,128)(2,1)S(1)} %get-tuple-element.367), channel_id=1, source_target_pairs={{0,4},{4,8},{8,12},{12,16},{16,20},{20,24},{24,28},{28,32},{32,36}... | collective-permute-start | bytes 786440 | tf_op jit(solution)/shard_map/while/body/eval_jaxpr/ppermute | solution.py:17
  278.0 11.0 %collective-permute-start = (bf16[256,512]{0,1:T(8,128)(2,1)S(1)}, bf16[256,512]{0,1:T(8,128)(2,1)S(1)}, u32[]{:S(2)}, u32[]{:S(2)}) collective-permute-start(bf16[256,512]{0,1:T(8,128)(2,1)S(1)} %get-tuple-element.367), channel_id=1, source_target_pairs={{0,4},{4,8},{8,12},{12,16},{16,20},{20,24},{24,28},{28,32},{32,36}... | collective-permute-start | bytes 786440 | tf_op jit(solution)/shard_map/while/body/eval_jaxpr/ppermute | solution.py:17
  290.6 11.0 %collective-permute-start = (bf16[256,512]{0,1:T(8,128)(2,1)S(1)}, bf16[256,512]{0,1:T(8,128)(2,1)S(1)}, u32[]{:S(2)}, u32[]{:S(2)}) collective-permute-start(bf16[256,512]{0,1:T(8,128)(2,1)S(1)} %get-tuple-element.367), channel_id=1, source_target_pairs={{0,4},{4,8},{8,12},{12,16},{16,20},{20,24},{24,28},{28,32},{32,36}... | collective-permute-start | bytes 786440 | tf_op jit(solution)/shard_map/while/body/eval_jaxpr/ppermute | solution.py:17
  303.3 11.0 %collective-permute-start = (bf16[256,512]{0,1:T(8,128)(2,1)S(1)}, bf16[256,512]{0,1:T(8,128)(2,1)S(1)}, u32[]{:S(2)}, u32[]{:S(2)}) collective-permute-start(bf16[256,512]{0,1:T(8,128)(2,1)S(1)} %get-tuple-element.367), channel_id=1, source_target_pairs={{0,4},{4,8},{8,12},{12,16},{16,20},{20,24},{24,28},{28,32},{32,36}... | collective-permute-start | bytes 786440 | tf_op jit(solution)/shard_map/while/body/eval_jaxpr/ppermute | solution.py:17
  316.0 11.0 %collective-permute-start = (bf16[256,512]{0,1:T(8,128)(2,1)S(1)}, bf16[256,512]{0,1:T(8,128)(2,1)S(1)}, u32[]{:S(2)}, u32[]{:S(2)}) collective-permute-start(bf16[256,512]{0,1:T(8,128)(2,1)S(1)} %get-tuple-element.367), channel_id=1, source_target_pairs={{0,4},{4,8},{8,12},{12,16},{16,20},{20,24},{24,28},{28,32},{32,36}... | collective-permute-start | bytes 786440 | tf_op jit(solution)/shard_map/while/body/eval_jaxpr/ppermute | solution.py:17
  328.7 11.0 %collective-permute-start = (bf16[256,512]{0,1:T(8,128)(2,1)S(1)}, bf16[256,512]{0,1:T(8,128)(2,1)S(1)}, u32[]{:S(2)}, u32[]{:S(2)}) collective-permute-start(bf16[256,512]{0,1:T(8,128)(2,1)S(1)} %get-tuple-element.367), channel_id=1, source_target_pairs={{0,4},{4,8},{8,12},{12,16},{16,20},{20,24},{24,28},{28,32},{32,36}... | collective-permute-start | bytes 786440 | tf_op jit(solution)/shard_map/while/body/eval_jaxpr/ppermute | solution.py:17
  341.3 11.0 %collective-permute-start = (bf16[256,512]{0,1:T(8,128)(2,1)S(1)}, bf16[256,512]{0,1:T(8,128)(2,1)S(1)}, u32[]{:S(2)}, u32[]{:S(2)}) collective-permute-start(bf16[256,512]{0,1:T(8,128)(2,1)S(1)} %get-tuple-element.367), channel_id=1, source_target_pairs={{0,4},{4,8},{8,12},{12,16},{16,20},{20,24},{24,28},{28,32},{32,36}... | collective-permute-start | bytes 786440 | tf_op jit(solution)/shard_map/while/body/eval_jaxpr/ppermute | solution.py:17
  354.0 11.0 %collective-permute-start = (bf16[256,512]{0,1:T(8,128)(2,1)S(1)}, bf16[256,512]{0,1:T(8,128)(2,1)S(1)}, u32[]{:S(2)}, u32[]{:S(2)}) collective-permute-start(bf16[256,512]{0,1:T(8,128)(2,1)S(1)} %get-tuple-element.367), channel_id=1, source_target_pairs={{0,4},{4,8},{8,12},{12,16},{16,20},{20,24},{24,28},{28,32},{32,36}... | collective-permute-start | bytes 786440 | tf_op jit(solution)/shard_map/while/body/eval_jaxpr/ppermute | solution.py:17
  366.7 11.0 %collective-permute-start = (bf16[256,512]{0,1:T(8,128)(2,1)S(1)}, bf16[256,512]{0,1:T(8,128)(2,1)S(1)}, u32[]{:S(2)}, u32[]{:S(2)}) collective-permute-start(bf16[256,512]{0,1:T(8,128)(2,1)S(1)} %get-tuple-element.367), channel_id=1, source_target_pairs={{0,4},{4,8},{8,12},{12,16},{16,20},{20,24},{24,28},{28,32},{32,36}... | collective-permute-start | bytes 786440 | tf_op jit(solution)/shard_map/while/body/eval_jaxpr/ppermute | solution.py:17
  379.4 11.0 %collective-permute-start = (bf16[256,512]{0,1:T(8,128)(2,1)S(1)}, bf16[256,512]{0,1:T(8,128)(2,1)S(1)}, u32[]{:S(2)}, u32[]{:S(2)}) collective-permute-start(bf16[256,512]{0,1:T(8,128)(2,1)S(1)} %get-tuple-element.367), channel_id=1, source_target_pairs={{0,4},{4,8},{8,12},{12,16},{16,20},{20,24},{24,28},{28,32},{32,36}... | collective-permute-start | bytes 786440 | tf_op jit(solution)/shard_map/while/body/eval_jaxpr/ppermute | solution.py:17
  392.0 11.0 %collective-permute-start = (bf16[256,512]{0,1:T(8,128)(2,1)S(1)}, bf16[256,512]{0,1:T(8,128)(2,1)S(1)}, u32[]{:S(2)}, u32[]{:S(2)}) collective-permute-start(bf16[256,512]{0,1:T(8,128)(2,1)S(1)} %get-tuple-element.367), channel_id=1, source_target_pairs={{0,4},{4,8},{8,12},{12,16},{16,20},{20,24},{24,28},{28,32},{32,36}... | collective-permute-start | bytes 786440 | tf_op jit(solution)/shard_map/while/body/eval_jaxpr/ppermute | solution.py:17
  404.7 11.0 %collective-permute-start = (bf16[256,512]{0,1:T(8,128)(2,1)S(1)}, bf16[256,512]{0,1:T(8,128)(2,1)S(1)}, u32[]{:S(2)}, u32[]{:S(2)}) collective-permute-start(bf16[256,512]{0,1:T(8,128)(2,1)S(1)} %get-tuple-element.367), channel_id=1, source_target_pairs={{0,4},{4,8},{8,12},{12,16},{16,20},{20,24},{24,28},{28,32},{32,36}... | collective-permute-start | bytes 786440 | tf_op jit(solution)/shard_map/while/body/eval_jaxpr/ppermute | solution.py:17
  419.1 11.7 %all-to-all-start = ((bf16[4,64,768]{2,1,0:T(8,128)(2,1)}), bf16[4,64,768]{2,1,0:T(8,128)(2,1)S(1)}, u32[]{:S(2)}, u32[]{:S(2)}) async-start(bf16[4,64,768]{2,1,0:T(8,128)(2,1)} %all_to_all.14), calls=%async_computation | async-start | bytes 786432 | tf_op jit(solution)/shard_map/all_to_all | solution.py:103
where the time goes:
time: 436 us; the launch traced here: 432 us
  waiting for transfers between devices  291 us (67%)
  starting transfers between devices  65.7 us (15%)
  matrix products  40.8 us (9%)
  other arithmetic  20 us (5%)
  local copies, waits for them, and re-layouts  10.1 us (2%)
    ppermute x32, waiting for transfers between devices, shifted(): return lax.ppermute(block, axis, route)  285 us
    ppermute x32, starting transfers between devices, shifted(): return lax.ppermute(block, axis, route)  61.5 us
    dot_general x33, matrix products, attend_block(): jnp.einsum('hgqk,khd->qhgd', weights.astype(jnp.bfloat16), value_heads, p...  25.6 us
    dot_general x33, matrix products, attend_block(): jnp.einsum('qhgd,khd->hgqk', queries_local, key_heads, preferred_element_...  15.2 us
    reduce_sum x33, other arithmetic, attend_block(): totals = totals * factor + jnp.sum(weights, axis=-1)  9.68 us
  transfers between devices with their start and end apart: 33, of which 33 were waited for; matrix products, arithmetic and copies ran while one was open for 2% of the time, Pallas kernels for 0%

commit v1 on v0

v1 whole, which is shorter than its diff:
```python
import math

import jax
import jax.numpy as jnp
from jax import lax
from jax.experimental import pallas as pl
from jax.experimental.pallas import tpu as pltpu
from jax.sharding import PartitionSpec as P

MESH = pl.DeviceIdType.MESH
HEAD_DIM = 128
GROUP = 3
ROWS = 256
CHUNK = 256
DOCS = 16
NEG = -1e30
SCALE = 1.0 / math.sqrt(HEAD_DIM)
TO_EXP2 = SCALE / math.log(2.0)

ARRIVALS = (
    (
        (63, 0, 2, 4, 6, 8, 10, 12),
        (63, 1, 3, 5, 7, 9, 11, 13),
        (30, 16, 0, 2, 4, 6, 8, 10),
        (31, 17, 1, 3, 5, 7, 9, 11),
        (28, 30, 16, 0, 2, 4, 6, 8),
        (29, 31, 18, 1, 3, 5, 7, 9),
        (26, 28, 30, 21, 0, 2, 4, 6),
        (27, 29, 31, 18, 1, 3, 5, 7),
        (24, 26, 19, 30, 40, 21, 2, 4),
        (25, 27, 17, 31, 16, 43, 3, 5),
        (46, 63, 46, 19, 18, 44, 21, 2),
        (47, 43, 63, 63, 63, 63, 63, 3),
    ),
    (
        (63, 63, 63, 63, 63, 63, 63, 0),
        (63, 63, 63, 63, 63, 63, 63, 1),
        (18, 20, 22, 24, 26, 28, 30, 16),
        (19, 21, 23, 25, 27, 29, 31, 17),
        (20, 22, 24, 26, 28, 30, 0, 18),
        (21, 23, 25, 27, 29, 31, 1, 19),
        (22, 24, 26, 28, 30, 0, 17, 20),
        (23, 25, 27, 29, 31, 1, 18, 21),
        (38, 40, 28, 43, 45, 17, 20, 22),
        (39, 41, 29, 44, 46, 18, 19, 23),
        (40, 42, 63, 45, 17, 20, 16, 63),
        (41, 63, 44, 63, 63, 19, 63, 63),
    ),
    (
        (16, 18, 20, 22, 24, 26, 28, 30),
        (17, 19, 21, 23, 25, 27, 29, 31),
        (32, 34, 36, 38, 22, 24, 26, 28),
        (33, 35, 37, 20, 23, 25, 27, 29),
        (34, 36, 38, 40, 42, 22, 24, 26),
        (35, 37, 39, 41, 21, 23, 25, 27),
        (36, 38, 40, 39, 43, 45, 22, 24),
        (37, 39, 41, 16, 44, 46, 23, 25),
        (42, 46, 42, 42, 41, 42, 47, 46),
        (43, 47, 43, 17, 19, 16, 45, 47),
        (44, 45, 47, 46, 20, 47, 44, 63),
        (45, 44, 45, 47, 47, 63, 46, 63),
    ),
)
NONE = 63
SLOTS = len(ARRIVALS[0])
PER_WORD = 5
BITS = 6


def departures(link):
    table = ARRIVALS[link]
    if link == 0:
        return [[row[(z + 1) % 8] for z in range(8)] for row in table]
    if link == 1:
        return [[row[(z - 1) % 8] for z in range(8)] for row in table]
    return [[v if v == NONE else v - 16 for v in row] for row in table]


def packed_words(table, z):
    words = []
    for first in range(0, SLOTS, PER_WORD):
        word = jnp.int32(0)
        for k in range(8):
            const = 0
            for i, row in enumerate(table[first : first + PER_WORD]):
                const += row[k] << (BITS * i)
            word = jnp.where(z == k, jnp.int32(const), word)
        words.append(word)
    return words


def look_up(words, slot):
    word = words[-1]
    for i in range(len(words) - 2, -1, -1):
        word = jnp.where(slot < (i + 1) * PER_WORD, words[i], word)
    return lax.shift_right_logical(word, BITS * lax.rem(slot, PER_WORD)) & (2**BITS - 1)


def kernel(
    q_ref, k_ref, v_ref, len_ref, out_ref, log_ref,
    buf, q_other, q_t, acc, peak, total, starts, staged, log_out, log_in,
    send_sem, recv_sem, trade_send, trade_recv, out_send, out_recv, log_sem,
):
    ctx, x = lax.axis_index("ctx"), lax.axis_index("tp")
    core, z, y = lax.rem(ctx, 2), lax.rem(ctx // 2, 8), ctx // 16

    def device(dy=0, dz=0, dcore=0, dx=0):
        yy, zz = lax.rem(y + dy + 8, 8), lax.rem(z + dz + 8, 8)
        return ((yy * 8 + zz) * 2 + lax.rem(core + dcore, 2), lax.rem(x + dx, 4))

    link_to = (device(dz=1), device(dz=-1), device(dy=1))

    barrier = pltpu.get_barrier_semaphore()
    senders = [device(dz=-1), device(dz=1), device(dy=-1)]
    senders += [device(dcore=h, dx=dx) for h in range(2) for dx in range(4) if h + dx]
    for d in senders:
        pl.semaphore_signal(barrier, inc=1, device_id=d, device_id_type=MESH)

    own = z * 2
    mine = pl.ds(pl.multiple_of(core * HEAD_DIM, HEAD_DIM), HEAD_DIM)
    theirs = pl.ds(pl.multiple_of((1 - core) * HEAD_DIM, HEAD_DIM), HEAD_DIM)
    width = GROUP * HEAD_DIM
    theirs_q = pl.ds(pl.multiple_of((1 - core) * width, HEAD_DIM), width)
    buf[own, :CHUNK, :] = k_ref[:, mine]
    buf[own, CHUNK:, :] = v_ref[:, mine]

    rx = [packed_words(ARRIVALS[link], z) for link in range(3)]
    tx = [packed_words(departures(link), z) for link in range(3)]

    pl.semaphore_wait(barrier, len(senders))

    other = device(dcore=1)

    def trade(i, src, dst):
        return pltpu.make_async_remote_copy(
            src_ref=src, dst_ref=dst, send_sem=trade_send.at[i], recv_sem=trade_recv.at[i],
            device_id=other, device_id_type=MESH,
        )

    trades = [
        trade(0, k_ref.at[:, theirs], buf.at[own + 1, pl.ds(0, CHUNK)]),
        trade(1, v_ref.at[:, theirs], buf.at[own + 1, pl.ds(CHUNK, CHUNK)]),
        trade(2, q_ref.at[:, theirs_q], q_other),
    ]

    def move(link, slot, chunk):
        landing = chunk + 16 if link == 2 else chunk
        return pltpu.make_async_remote_copy(
            src_ref=buf.at[chunk], dst_ref=buf.at[landing],
            send_sem=send_sem.at[link, slot], recv_sem=recv_sem.at[link, slot],
            device_id=link_to[link], device_id_type=MESH,
        )

    def send(slot):
        for link in range(3):
            chunk = look_up(tx[link], slot)

            @pl.when(chunk != NONE)
            def _(link=link, chunk=chunk):
                move(link, slot, chunk).start()

    for t in trades:
        t.start()
    send(jnp.int32(0))

    for half in range(2):
        base = (ctx - core) * ROWS + lax.rem(core + half, 2) * ROWS
        q_pos = base + lax.broadcasted_iota(jnp.int32, (1, ROWS), 1)
        start = jnp.zeros((1, ROWS), jnp.int32)
        end = jnp.int32(0)
        for i in range(DOCS):
            end = end + len_ref[i]
            start = jnp.where(q_pos >= end, end, start)
        starts[half : half + 1, :] = start
        starts[2 + half : 3 + half, :] = q_pos

    for g in range(GROUP):
        cols = pl.ds(pl.multiple_of(core * width + g * HEAD_DIM, HEAD_DIM), HEAD_DIM)
        q_t[:, 2 * g * ROWS : (2 * g + 1) * ROWS] = q_ref[:, cols].T

    trades[0].wait_recv()
    trades[1].wait_recv()
    send(jnp.int32(1))
    trades[2].wait_recv()
    for g in range(GROUP):
        q_t[:, (2 * g + 1) * ROWS : (2 * g + 2) * ROWS] = q_other[
            :, g * HEAD_DIM : (g + 1) * HEAD_DIM
        ].T

    def attend(chunks, first):
        keys, values, positions = [], [], []
        for chunk, base in chunks:
            keys.append(buf[chunk, :CHUNK, :])
            values.append(buf[chunk, CHUNK:, :].T)
            positions.append(base + lax.broadcasted_iota(jnp.int32, (CHUNK, ROWS), 0))
        for b in range(2 * GROUP):
            half = b % 2
            cols = slice(b * ROWS, (b + 1) * ROWS)
            start = starts[half : half + 1, :]
            scores = []
            for k, pos in zip(keys, positions):
                s = jnp.dot(k, q_t[:, cols], preferred_element_type=jnp.float32)
                allowed = pos >= start
                if first:
                    allowed = allowed & (pos <= starts[2 + half : 3 + half, :])
                scores.append(jnp.where(allowed, s, NEG))
            top = scores[0]
            for s in scores[1:]:
                top = jnp.maximum(top, s)
            top = jnp.max(top, axis=0, keepdims=True)
            if not first:
                before = peak[b : b + 1, :]
                top = jnp.maximum(top, before)
                factor = jnp.exp2((before - top) * TO_EXP2)
            summed, update = None, None
            for s, v in zip(scores, values):
                w = jnp.exp2((s - top) * TO_EXP2)
                part = jnp.dot(v, w.astype(jnp.bfloat16), preferred_element_type=jnp.float32)
                summed = w if summed is None else summed + w
                update = part if update is None else update + part
            summed = jnp.sum(summed, axis=0, keepdims=True)
            if not first:
                summed = summed + total[b : b + 1, :] * factor
                update = update + acc[:, cols] * factor
            peak[b : b + 1, :] = top
            total[b : b + 1, :] = summed
            acc[:, cols] = update

    def base_of(chunk):
        back, s, part = chunk // 16, lax.rem(chunk // 2, 8), lax.rem(chunk, 2)
        base = (((y - back) * 8 + s) * 2 + lax.rem(part + core, 2)) * ROWS
        return jnp.where(chunk == NONE, -ROWS, base)

    attend([(own, base_of(own)), (own + 1, base_of(own + 1))], True)

    def step(slot, carry):
        chunks = []
        for link in range(3):
            chunk = look_up(rx[link], slot)
            safe = jnp.where(chunk == NONE, own, chunk)

            @pl.when(chunk != NONE)
            def _(link=link, safe=safe):
                pltpu.make_async_remote_copy(
                    src_ref=buf.at[safe], dst_ref=buf.at[safe],
                    send_sem=send_sem.at[link, slot], recv_sem=recv_sem.at[link, slot],
                    device_id=link_to[link], device_id_type=MESH,
                ).wait_recv()

            chunks.append((safe, base_of(chunk)))

        @pl.when(slot + 2 < SLOTS)
        def _():
            send(slot + 2)

        attend(chunks, False)
        return carry

    lax.fori_loop(0, SLOTS, step, 0)

    for b in range(2 * GROUP):
        g, half = b // 2, b % 2
        sums = total[b : b + 1, :]
        o = (acc[:, b * ROWS : (b + 1) * ROWS] / sums).T
        staged[half * ROWS : (half + 1) * ROWS, g * HEAD_DIM : (g + 1) * HEAD_DIM] = o.astype(
            jnp.bfloat16
        )
        log_out[half, g : g + 1, :] = peak[b : b + 1, :] * SCALE + jnp.log(sums)

    share = ROWS // 4
    spot = pl.ds(pl.multiple_of((2 * x + core) * width, HEAD_DIM), width)
    sends = []
    for half in range(2):
        for dx in range(4):
            if half + dx == 0:
                continue
            to = lax.rem(x + dx, 4)
            copy = pltpu.make_async_remote_copy(
                src_ref=staged.at[pl.ds(pl.multiple_of(half * ROWS + to * share, share), share)],
                dst_ref=out_ref.at[:, spot],
                send_sem=out_send.at[half, dx], recv_sem=out_recv.at[half, dx],
                device_id=device(dcore=half, dx=dx), device_id_type=MESH,
            )
            copy.start()
            sends.append(copy)
    log_copy = pltpu.make_async_remote_copy(
        src_ref=log_out.at[1], dst_ref=log_in, send_sem=log_sem.at[0], recv_sem=log_sem.at[1],
        device_id=other, device_id_type=MESH,
    )
    log_copy.start()
    out_ref[:, spot] = staged[pl.ds(pl.multiple_of(x * share, share), share), :]
    log_copy.wait()
    near, far = log_out[0, :GROUP, :], log_in[:GROUP, :]
    log_ref[:GROUP, :] = jnp.where(core == 0, near, far)
    log_ref[GROUP:, :] = jnp.where(core == 0, far, near)

    for t in trades:
        t.wait_send()

    def drain(slot, carry):
        for link in range(3):
            chunk = look_up(tx[link], slot)

            @pl.when(chunk != NONE)
            def _(link=link, chunk=chunk):
                move(link, slot, chunk).wait_send()

        return carry

    lax.fori_loop(0, SLOTS, drain, 0)
    for copy in sends:
        copy.wait()


def on_device(queries, keys, values, doc_lengths):
    columns = 4 * queries.shape[1]
    dma = pltpu.SemaphoreType.DMA
    vmem = pl.BlockSpec(memory_space=pltpu.VMEM)
    return pl.pallas_call(
        kernel,
        out_shape=(
            jax.ShapeDtypeStruct((ROWS // 4, columns), jnp.bfloat16),
            jax.ShapeDtypeStruct((2 * GROUP, ROWS), jnp.float32),
        ),
        in_specs=[vmem, vmem, vmem, pl.BlockSpec(memory_space=pltpu.SMEM)],
        out_specs=(vmem, vmem),
        scratch_shapes=[
            pltpu.VMEM((48, 2 * CHUNK, HEAD_DIM), jnp.bfloat16),
            pltpu.VMEM((ROWS, GROUP * HEAD_DIM), jnp.bfloat16),
            pltpu.VMEM((HEAD_DIM, 2 * GROUP * ROWS), jnp.bfloat16),
            pltpu.VMEM((HEAD_DIM, 2 * GROUP * ROWS), jnp.float32),
            pltpu.VMEM((8, ROWS), jnp.float32),
            pltpu.VMEM((8, ROWS), jnp.float32),
            pltpu.VMEM((8, ROWS), jnp.int32),
            pltpu.VMEM((2 * ROWS, GROUP * HEAD_DIM), jnp.bfloat16),
            pltpu.VMEM((2, 8, ROWS), jnp.float32),
            pltpu.VMEM((8, ROWS), jnp.float32),
            dma((3, SLOTS)),
            dma((3, SLOTS)),
            dma((3,)),
            dma((3,)),
            dma((2, 4)),
            dma((2, 4)),
            dma((2,)),
        ],
        compiler_params=pltpu.CompilerParams(
            collective_id=0, has_side_effects=True, vmem_limit_bytes=48 * 2**20
        ),
        cost_estimate=pl.CostEstimate(
            flops=8 * 10**9, bytes_accessed=2 * 10**6, transcendentals=14 * 10**6
        ),
    )(queries, keys, values, doc_lengths)


def solution(mesh):
    in_specs = (P("ctx", "tp"), P("ctx", "tp"), P("ctx", "tp"), P())
    out_specs = (P(("ctx", "tp"), None), P("tp", "ctx"))
    return jax.shard_map(
        on_device, mesh=mesh, in_specs=in_specs, out_specs=out_specs, check_vma=False
    )
```

time: 436 us -> 66.3 us (0.15)
  the two profiles are of different devices: /device:TPU:32 before, /device:TPU:1 now
where the time goes in v1:
time: 66.3 us; the launch traced here: 66 us
  Pallas kernels  60.6 us (91%)
  local copies, waits for them, and re-layouts  4.8 us (7%)
    pallas_call x1, Pallas kernels, on_device(): pl.pallas_call(kernel, out_shape=(jax.ShapeDtypeStruct((ROWS // 4, column...  60.6 us
    unnamed x10, local copies, waits for them, and re-layouts  4.8 us

profile of v1, /device:TPU:1, one launch (start us, length us, event | category | flops | bytes accessed | tf_op | source)
XLA Modules:
  0.0 66.0 jit_solution(13938953247600679261)
XLA Ops:
  0.6 0.0 copy-start
  0.6 1.0 %copy-done = bf16[256,768]{1,0:T(8,128)(2,1)S(1)} copy-done((bf16[256,768]{1,0:T(8,128)(2,1)S(1)}, bf16[256,768]{1,0:T(8,128)(2,1)}, u32[]{:S(2)}) %copy-start) | copy-done | bytes 393240
  1.6 0.0 copy-start.1
  1.6 0.9 %copy-done.1 = bf16[256,256]{1,0:T(8,128)(2,1)S(1)} copy-done((bf16[256,256]{1,0:T(8,128)(2,1)S(1)}, bf16[256,256]{1,0:T(8,128)(2,1)}, u32[]{:S(2)}) %copy-start.1) | copy-done | bytes 131096
  2.5 0.0 copy-start.2
  2.5 0.9 %copy-done.2 = bf16[256,256]{1,0:T(8,128)(2,1)S(1)} copy-done((bf16[256,256]{1,0:T(8,128)(2,1)S(1)}, bf16[256,256]{1,0:T(8,128)(2,1)}, u32[]{:S(2)}) %copy-start.2) | copy-done | bytes 131096
  3.4 0.0 copy-start.3
  3.4 0.7 copy-done.3
  4.1 60.6 %shard_map.59 = (bf16[64,3072]{1,0:T(8,128)(2,1)S(1)}, f32[6,256]{1,0:T(8,128)S(1)}) custom-call(bf16[256,768]{1,0:T(8,128)(2,1)S(1)} %copy-done, bf16[256,256]{1,0:T(8,128)(2,1)S(1)} %copy-done.1, bf16[256,256]{1,0:T(8,128)(2,1)S(1)} %copy-done.2, s32[16]{0:T(128)S(1)} %copy-done.3), custom_call_target="tpu_custom_call" | custom-call | flops 8000000000 | bytes 2000000 | tf_op jit(solution)/shard_map/pallas_call | solution.py:319
  64.7 0.7 %copy.8 = bf16[64,3072]{1,0:T(8,128)(2,1)} copy(bf16[64,3072]{1,0:T(8,128)(2,1)S(1)} %get-tuple-element.4) | data formatting | bytes 786432
  65.5 0.6 copy.9
Async XLA Ops:
  0.6 1.0 %copy-start = (bf16[256,768]{1,0:T(8,128)(2,1)S(1)}, bf16[256,768]{1,0:T(8,128)(2,1)}, u32[]{:S(2)}) copy-start(bf16[256,768]{1,0:T(8,128)(2,1)} %q_ref.1) | copy-start | bytes 1179652
  1.6 0.9 %copy-start.1 = (bf16[256,256]{1,0:T(8,128)(2,1)S(1)}, bf16[256,256]{1,0:T(8,128)(2,1)}, u32[]{:S(2)}) copy-start(bf16[256,256]{1,0:T(8,128)(2,1)} %k_ref.1) | copy-start | bytes 393220
  2.5 0.9 %copy-start.2 = (bf16[256,256]{1,0:T(8,128)(2,1)S(1)}, bf16[256,256]{1,0:T(8,128)(2,1)}, u32[]{:S(2)}) copy-start(bf16[256,256]{1,0:T(8,128)(2,1)} %v_ref.1) | copy-start | bytes 393220
  3.4 0.7 copy-start.3

commit v2 on v1

v2 whole, which is shorter than its diff:
```python
import math

import jax
import jax.numpy as jnp
from jax import lax
from jax.experimental import pallas as pl
from jax.experimental.pallas import tpu as pltpu
from jax.sharding import PartitionSpec as P

MESH = pl.DeviceIdType.MESH
HEAD_DIM = 128
GROUP = 3
ROWS = 256
CHUNK = 256
DOCS = 16
NEG = -1e30
APART = 2.0**20
SCALE = 1.0 / math.sqrt(HEAD_DIM)
TO_EXP2 = SCALE / math.log(2.0)

ARRIVALS = (
    (
        (63, 0, 2, 4, 6, 8, 10, 12),
        (63, 1, 3, 5, 7, 9, 11, 13),
        (30, 16, 0, 2, 4, 6, 8, 10),
        (31, 17, 1, 3, 5, 7, 9, 11),
        (28, 30, 16, 0, 2, 4, 6, 8),
        (29, 31, 18, 1, 3, 5, 7, 9),
        (26, 28, 30, 21, 0, 2, 4, 6),
        (27, 29, 31, 18, 1, 3, 5, 7),
        (24, 26, 19, 30, 40, 21, 2, 4),
        (25, 27, 17, 31, 16, 43, 3, 5),
        (46, 63, 46, 19, 18, 44, 21, 2),
        (47, 43, 63, 63, 63, 63, 63, 3),
    ),
    (
        (63, 63, 63, 63, 63, 63, 63, 0),
        (63, 63, 63, 63, 63, 63, 63, 1),
        (18, 20, 22, 24, 26, 28, 30, 16),
        (19, 21, 23, 25, 27, 29, 31, 17),
        (20, 22, 24, 26, 28, 30, 0, 18),
        (21, 23, 25, 27, 29, 31, 1, 19),
        (22, 24, 26, 28, 30, 0, 17, 20),
        (23, 25, 27, 29, 31, 1, 18, 21),
        (38, 40, 28, 43, 45, 17, 20, 22),
        (39, 41, 29, 44, 46, 18, 19, 23),
        (40, 42, 63, 45, 17, 20, 16, 63),
        (41, 63, 44, 63, 63, 19, 63, 63),
    ),
    (
        (16, 18, 20, 22, 24, 26, 28, 30),
        (17, 19, 21, 23, 25, 27, 29, 31),
        (32, 34, 36, 38, 22, 24, 26, 28),
        (33, 35, 37, 20, 23, 25, 27, 29),
        (34, 36, 38, 40, 42, 22, 24, 26),
        (35, 37, 39, 41, 21, 23, 25, 27),
        (36, 38, 40, 39, 43, 45, 22, 24),
        (37, 39, 41, 16, 44, 46, 23, 25),
        (42, 46, 42, 42, 41, 42, 47, 46),
        (43, 47, 43, 17, 19, 16, 45, 47),
        (44, 45, 47, 46, 20, 47, 44, 63),
        (45, 44, 45, 47, 47, 63, 46, 63),
    ),
)
NONE = 63
SLOTS = len(ARRIVALS[0])
PER_WORD = 5
BITS = 6


def departures(link):
    table = ARRIVALS[link]
    if link == 0:
        return [[row[(z + 1) % 8] for z in range(8)] for row in table]
    if link == 1:
        return [[row[(z - 1) % 8] for z in range(8)] for row in table]
    return [[v if v == NONE else v - 16 for v in row] for row in table]


def packed_words(table, z):
    words = []
    for first in range(0, SLOTS, PER_WORD):
        word = jnp.int32(0)
        for k in range(8):
            const = 0
            for i, row in enumerate(table[first : first + PER_WORD]):
                const += row[k] << (BITS * i)
            word = jnp.where(z == k, jnp.int32(const), word)
        words.append(word)
    return words


def look_up(words, slot):
    word = words[-1]
    for i in range(len(words) - 2, -1, -1):
        word = jnp.where(slot < (i + 1) * PER_WORD, words[i], word)
    return lax.shift_right_logical(word, BITS * lax.rem(slot, PER_WORD)) & (2**BITS - 1)


def kernel(
    q_ref, k_ref, v_ref, len_ref, out_ref, log_ref,
    buf, q_near, q_far, q_all, acc, peak, bounds, lengths, staged, log_out, log_in,
    send_sem, recv_sem, local_sem, trade_send, trade_recv, out_send, out_recv, log_sem,
):
    ctx, x = lax.axis_index("ctx"), lax.axis_index("tp")
    core, z, y = lax.rem(ctx, 2), lax.rem(ctx // 2, 8), ctx // 16

    def device(dy=0, dz=0, dcore=0, dx=0):
        yy, zz = lax.rem(y + dy + 8, 8), lax.rem(z + dz + 8, 8)
        return ((yy * 8 + zz) * 2 + lax.rem(core + dcore, 2), lax.rem(x + dx, 4))

    link_to = (device(dz=1), device(dz=-1), device(dy=1))

    barrier = pltpu.get_barrier_semaphore()
    senders = [device(dz=-1), device(dz=1), device(dy=-1)]
    senders += [device(dcore=h, dx=dx) for h in range(2) for dx in range(4) if h + dx]
    for d in senders:
        pl.semaphore_signal(barrier, inc=1, device_id=d, device_id_type=MESH)

    own = z * 2
    width = GROUP * HEAD_DIM
    mine = pl.ds(pl.multiple_of(core * HEAD_DIM, HEAD_DIM), HEAD_DIM)
    theirs = pl.ds(pl.multiple_of((1 - core) * HEAD_DIM, HEAD_DIM), HEAD_DIM)
    mine_q = pl.ds(pl.multiple_of(core * width, HEAD_DIM), width)
    theirs_q = pl.ds(pl.multiple_of((1 - core) * width, HEAD_DIM), width)
    local = [
        pltpu.make_async_copy(src, dst, local_sem.at[i])
        for i, (src, dst) in enumerate(
            (
                (k_ref.at[:, mine], buf.at[own, pl.ds(0, CHUNK)]),
                (v_ref.at[:, mine], buf.at[own, pl.ds(CHUNK, CHUNK)]),
                (q_ref.at[:, mine_q], q_near),
                (len_ref, lengths),
            )
        )
    ]
    for copy in local:
        copy.start()

    rx = [packed_words(ARRIVALS[link], z) for link in range(3)]
    tx = [packed_words(departures(link), z) for link in range(3)]

    other = device(dcore=1)

    def trade(i, src, dst):
        return pltpu.make_async_remote_copy(
            src_ref=src, dst_ref=dst, send_sem=trade_send.at[i], recv_sem=trade_recv.at[i],
            device_id=other, device_id_type=MESH,
        )

    trades = [
        trade(0, k_ref.at[:, theirs], buf.at[own + 1, pl.ds(0, CHUNK)]),
        trade(1, v_ref.at[:, theirs], buf.at[own + 1, pl.ds(CHUNK, CHUNK)]),
        trade(2, q_ref.at[:, theirs_q], q_far),
    ]

    def move(link, slot, chunk):
        landing = chunk + 16 if link == 2 else chunk
        return pltpu.make_async_remote_copy(
            src_ref=buf.at[chunk], dst_ref=buf.at[landing],
            send_sem=send_sem.at[link, slot], recv_sem=recv_sem.at[link, slot],
            device_id=link_to[link], device_id_type=MESH,
        )

    def leaving(link, slot):
        chunk = look_up(tx[link], slot)
        there = (chunk != NONE) & (chunk // 16 <= y)
        return chunk, (there & (y < 7)) if link == 2 else there

    def send(slot):
        for link in range(3):
            chunk, there = leaving(link, slot)

            @pl.when(there)
            def _(link=link, chunk=chunk):
                move(link, slot, chunk).start()

    pl.semaphore_wait(barrier, len(senders))
    trades[0].start()
    trades[1].start()
    local[0].wait()
    local[1].wait()
    send(jnp.int32(0))
    trades[2].start()

    local[3].wait()
    lane = lax.broadcasted_iota(jnp.int32, (1, HEAD_DIM), 1)
    starts = jnp.zeros((1, HEAD_DIM), jnp.int32)
    ends = jnp.zeros((1, HEAD_DIM), jnp.int32)
    end = jnp.int32(0)
    for i in range(DOCS):
        starts = jnp.where(lane == i, end, starts)
        end = end + lengths[i]
        ends = jnp.where(lane == i, end, ends)
    bounds[0:1, :] = starts
    bounds[1:2, :] = ends

    def in_document(base):
        pos = base + lax.broadcasted_iota(jnp.int32, (CHUNK, HEAD_DIM), 0)
        return (pos >= bounds[0:1, :]) & (pos < bounds[1:2, :])

    q_base = [(ctx - core + lax.rem(core + half, 2)) * ROWS for half in range(2)]
    for half in range(2):
        one_hot = jnp.where(in_document(q_base[half]), 1.0, 0.0).astype(jnp.bfloat16)
        for g in range(GROUP):
            b = 2 * g + half
            q_all[b * ROWS : (b + 1) * ROWS, HEAD_DIM:] = one_hot
    local[2].wait()
    trades[0].wait_recv()
    trades[1].wait_recv()
    send(jnp.int32(1))
    trades[2].wait_recv()
    for half, q_half in enumerate((q_near, q_far)):
        for g in range(GROUP):
            b = 2 * g + half
            q_all[b * ROWS : (b + 1) * ROWS, :HEAD_DIM] = q_half[
                :, g * HEAD_DIM : (g + 1) * HEAD_DIM
            ]

    halves = (slice(0, HEAD_DIM), slice(HEAD_DIM, 2 * HEAD_DIM))

    def load(chunks):
        keys, values = [], []
        for chunk, base in chunks:
            apart = jnp.where(in_document(base), 0.0, -APART).astype(jnp.bfloat16)
            keys.append(jnp.concatenate([buf[chunk, :CHUNK, :], apart], axis=1))
            ones = jnp.ones((CHUNK, HEAD_DIM), jnp.bfloat16)
            values.append(jnp.concatenate([buf[chunk, CHUNK:, :], ones], axis=1))
        return keys, jnp.concatenate(values, axis=0)

    def attend(b, keys, values, bases=None):
        rows = slice(b * ROWS, (b + 1) * ROWS)
        q = q_all[rows, :]
        scores = []
        for i, k in enumerate(keys):
            s = lax.dot_general(
                q, k, (((1,), (1,)), ((), ())), preferred_element_type=jnp.float32
            )
            if bases is not None:
                q_pos = q_base[b % 2] + lax.broadcasted_iota(jnp.int32, (ROWS, CHUNK), 0)
                k_pos = bases[i] + lax.broadcasted_iota(jnp.int32, (ROWS, CHUNK), 1)
                s = jnp.where(k_pos <= q_pos, s, NEG)
            scores += [s[:, h] for h in halves]
        top = scores[0]
        for s in scores[1:]:
            top = jnp.maximum(top, s)
        top = jnp.max(top, axis=1, keepdims=True)
        if bases is None:
            before = peak[rows, :]
            top = jnp.maximum(before, top)
            factor = jnp.exp2((before - top) * TO_EXP2)
        else:
            top = jnp.broadcast_to(top, (ROWS, HEAD_DIM))
        weights = [jnp.exp2((s - top) * TO_EXP2).astype(jnp.bfloat16) for s in scores]
        update = jnp.dot(
            jnp.concatenate(weights, axis=1), values, preferred_element_type=jnp.float32
        )
        peak[rows, :] = top
        for h in halves:
            acc[rows, h] = update[:, h] if bases is not None else acc[rows, h] * factor + update[:, h]

    def base_of(chunk, there):
        back, s, part = chunk // 16, lax.rem(chunk // 2, 8), lax.rem(chunk, 2)
        base = (((y - back) * 8 + s) * 2 + lax.rem(part + core, 2)) * ROWS
        return jnp.where(there, base, -ROWS)

    bases = q_base
    keys, values = load([(own, bases[0]), (own + 1, bases[1])])
    for b in range(2 * GROUP):
        attend(b, keys, values, bases)

    def arrived(slot):
        chunks = []
        for link in range(3):
            chunk = look_up(rx[link], slot)
            there = (chunk != NONE) & (chunk // 16 <= y)
            safe = jnp.where(there, chunk, own)

            @pl.when(there)
            def _(link=link, safe=safe):
                pltpu.make_async_remote_copy(
                    src_ref=buf.at[safe], dst_ref=buf.at[safe],
                    send_sem=send_sem.at[link, slot], recv_sem=recv_sem.at[link, slot],
                    device_id=link_to[link], device_id_type=MESH,
                ).wait_recv()

            chunks.append((safe, base_of(chunk, there)))
        return chunks

    def step(slot, carry):
        chunks = arrived(slot)

        @pl.when(slot + 2 < SLOTS)
        def _():
            send(slot + 2)

        keys, values = load(chunks)
        for b in range(2 * GROUP):
            attend(b, keys, values)
        return carry

    lax.fori_loop(0, SLOTS - 1, step, 0)

    share = ROWS // 4
    sends = []
    keys, values = load(arrived(jnp.int32(SLOTS - 1)))
    for b in range(2 * GROUP):
        attend(b, keys, values)
        g, half = b // 2, b % 2
        rows = slice(b * ROWS, (b + 1) * ROWS)
        staged[rows, :] = (acc[rows, :HEAD_DIM] / acc[rows, HEAD_DIM:]).astype(jnp.bfloat16)
        spot = pl.ds(pl.multiple_of((2 * x + core) * width + g * HEAD_DIM, HEAD_DIM), HEAD_DIM)
        for dx in range(4):
            to = lax.rem(x + dx, 4)
            piece = pl.ds(pl.multiple_of(b * ROWS + to * share, share), share)
            if half + dx == 0:
                out_ref[:, spot] = staged[piece, :]
                continue
            copy = pltpu.make_async_remote_copy(
                src_ref=staged.at[piece], dst_ref=out_ref.at[:, spot],
                send_sem=out_send.at[b, dx], recv_sem=out_recv.at[b, dx],
                device_id=device(dcore=half, dx=dx), device_id_type=MESH,
            )
            copy.start()
            sends.append(copy)

    for b in (1, 3, 5, 0, 2, 4):
        rows = slice(b * ROWS, (b + 1) * ROWS)
        log = (peak[rows, :] * SCALE + jnp.log(acc[rows, HEAD_DIM:])).T
        log_out[b % 2, b // 2 : b // 2 + 1, :] = log[:1, :]
        if b == 5:
            log_copy = pltpu.make_async_remote_copy(
                src_ref=log_out.at[1], dst_ref=log_in,
                send_sem=log_sem.at[0], recv_sem=log_sem.at[1],
                device_id=other, device_id_type=MESH,
            )
            log_copy.start()

    for t in trades:
        t.wait_send()

    def drain(slot, carry):
        for link in range(3):
            chunk, there = leaving(link, slot)

            @pl.when(there)
            def _(link=link, chunk=chunk):
                move(link, slot, chunk).wait_send()

        return carry

    lax.fori_loop(0, SLOTS, drain, 0)
    log_copy.wait()
    near, far = log_out[0, :GROUP, :], log_in[:GROUP, :]
    log_ref[:GROUP, :] = jnp.where(core == 0, near, far)
    log_ref[GROUP:, :] = jnp.where(core == 0, far, near)
    for copy in sends:
        copy.wait()


def on_device(queries, keys, values, doc_lengths):
    columns = 4 * queries.shape[1]
    dma = pltpu.SemaphoreType.DMA
    bf16, f32 = jnp.bfloat16, jnp.float32
    vmem = pl.BlockSpec(memory_space=pltpu.VMEM)
    return pl.pallas_call(
        kernel,
        out_shape=(
            jax.ShapeDtypeStruct((ROWS // 4, columns), bf16),
            jax.ShapeDtypeStruct((2 * GROUP, ROWS), f32),
        ),
        in_specs=[pl.BlockSpec(memory_space=pltpu.HBM)] * 4,
        out_specs=(vmem, vmem),
        scratch_shapes=[
            pltpu.VMEM((48, 2 * CHUNK, HEAD_DIM), bf16),
            pltpu.VMEM((ROWS, GROUP * HEAD_DIM), bf16),
            pltpu.VMEM((ROWS, GROUP * HEAD_DIM), bf16),
            pltpu.VMEM((2 * GROUP * ROWS, 2 * HEAD_DIM), bf16),
            pltpu.VMEM((2 * GROUP * ROWS, 2 * HEAD_DIM), f32),
            pltpu.VMEM((2 * GROUP * ROWS, HEAD_DIM), f32),
            pltpu.VMEM((8, HEAD_DIM), jnp.int32),
            pltpu.SMEM((DOCS,), jnp.int32),
            pltpu.VMEM((2 * GROUP * ROWS, HEAD_DIM), bf16),
            pltpu.VMEM((2, 8, ROWS), f32),
            pltpu.VMEM((8, ROWS), f32),
            dma((3, SLOTS)),
            dma((3, SLOTS)),
            dma((4,)),
            dma((3,)),
            dma((3,)),
            dma((2 * GROUP, 4)),
            dma((2 * GROUP, 4)),
            dma((2,)),
        ],
        compiler_params=pltpu.CompilerParams(
            collective_id=0, has_side_effects=True, vmem_limit_bytes=int(63.9 * 2**20)
        ),
        cost_estimate=pl.CostEstimate(
            flops=8 * 10**9, bytes_accessed=2 * 10**6, transcendentals=14 * 10**6
        ),
    )(queries, keys, values, doc_lengths)


def solution(mesh):
    in_specs = (P("ctx", "tp"), P("ctx", "tp"), P("ctx", "tp"), P())
    out_specs = (P(("ctx", "tp"), None), P("tp", "ctx"))
    return jax.shard_map(
        on_device, mesh=mesh, in_specs=in_specs, out_specs=out_specs, check_vma=False
    )
```

time: 66.3 us -> 60.6 us (0.914)
  the two profiles are of different devices: /device:TPU:1 before, /device:TPU:32 now
where the time goes in v2:
time: 60.6 us; the launch traced here: 59.8 us
  Pallas kernels  56.8 us (94%)
  local copies, waits for them, and re-layouts  2.37 us (4%)
  between operations  0.65 us (1%)
    pallas_call x1, Pallas kernels, on_device(): pl.pallas_call(kernel, out_shape=(jax.ShapeDtypeStruct((ROWS // 4, column...  56.8 us
    unnamed x4, local copies, waits for them, and re-layouts  2.37 us

profile of v2, /device:TPU:32, one launch (start us, length us, event | category | flops | bytes accessed | tf_op | source)
XLA Modules:
  0.0 59.8 jit_solution(9001758781841741117)
XLA Ops:
  0.6 56.8 %shard_map.59 = (bf16[64,3072]{1,0:T(8,128)(2,1)}, f32[6,256]{1,0:T(8,128)}) custom-call(bf16[256,768]{1,0:T(8,128)(2,1)} %q_ref.1, bf16[256,256]{1,0:T(8,128)(2,1)} %k_ref.1, bf16[256,256]{1,0:T(8,128)(2,1)} %v_ref.1, s32[16]{0:T(128)} %len_ref.1), custom_call_target="tpu_custom_call" | custom-call | flops 8000000000 | bytes 2000000 | tf_op jit(solution)/shard_map/pallas_call | solution.py:366
  57.4 0.0 copy-start
  57.4 1.8 %copy.8 = bf16[64,3072]{1,0:T(8,128)(2,1)} copy(bf16[64,3072]{1,0:T(8,128)(2,1)} %get-tuple-element.4) | data formatting | bytes 786432
  59.2 0.0 copy-done
  59.2 0.6 %copy.9 = f32[6,256]{1,0:T(8,128)} copy(f32[6,256]{1,0:T(8,128)S(1)} %copy-done) | data formatting | bytes 12288
Async XLA Ops:
  57.4 1.8 %copy-start = (f32[6,256]{1,0:T(8,128)S(1)}, f32[6,256]{1,0:T(8,128)}, u32[]{:S(2)}) copy-start(f32[6,256]{1,0:T(8,128)} %get-tuple-element.5) | copy-start | bytes 18436

commit v3 on v2

v3 whole, which is shorter than its diff:
```python
import math

import jax
import jax.numpy as jnp
from jax import lax
from jax.experimental import pallas as pl
from jax.experimental.pallas import tpu as pltpu
from jax.sharding import PartitionSpec as P

MESH = pl.DeviceIdType.MESH
HEAD_DIM = 128
GROUP = 3
ROWS = 256
CHUNK = 128
DOCS = 16
NEG = -1e30
APART = 2.0**20
SCALE = 1.0 / math.sqrt(HEAD_DIM)
TO_EXP2 = SCALE / math.log(2.0)

ARRIVALS = (
    (
        (127, 127, 127, 127, 127, 127, 127, 127),
        (127, 2, 127, 127, 127, 127, 127, 127),
        (127, 3, 5, 127, 127, 127, 127, 127),
        (127, 0, 6, 11, 127, 127, 127, 127),
        (127, 1, 4, 10, 14, 127, 127, 127),
        (127, 33, 7, 8, 15, 18, 20, 25),
        (127, 35, 2, 9, 13, 16, 23, 26),
        (127, 34, 0, 6, 12, 19, 22, 27),
        (127, 32, 1, 5, 10, 17, 21, 24),
        (61, 127, 3, 4, 8, 15, 18, 20),
        (60, 127, 37, 7, 9, 13, 16, 23),
        (62, 127, 39, 0, 11, 12, 19, 22),
        (63, 127, 34, 1, 6, 14, 17, 21),
        (57, 61, 35, 2, 4, 8, 15, 18),
        (58, 60, 33, 3, 7, 9, 13, 16),
        (59, 62, 36, 41, 5, 11, 12, 19),
        (56, 63, 127, 39, 1, 10, 14, 17),
        (52, 57, 61, 34, 0, 6, 8, 50),
        (55, 58, 60, 33, 3, 7, 9, 13),
        (54, 59, 62, 36, 2, 5, 11, 12),
        (53, 56, 63, 35, 39, 4, 10, 14),
        (50, 89, 93, 61, 34, 42, 6, 15),
        (48, 55, 58, 60, 37, 38, 7, 9),
        (51, 54, 57, 62, 36, 41, 5, 8),
        (94, 53, 127, 127, 32, 84, 4, 10),
        (95, 84, 89, 93, 82, 85, 91, 11),
        (127, 87, 90, 92, 35, 34, 38, 7),
        (127, 127, 127, 94, 127, 127, 42, 5),
        (127, 127, 127, 127, 127, 127, 127, 4),
        (127, 127, 127, 127, 127, 127, 127, 6),
    ),
    (
        (127, 127, 127, 127, 127, 127, 127, 127),
        (127, 127, 127, 127, 127, 127, 127, 127),
        (127, 127, 127, 127, 127, 127, 127, 127),
        (127, 127, 127, 127, 127, 127, 127, 127),
        (127, 127, 127, 127, 127, 127, 127, 127),
        (36, 127, 127, 127, 127, 127, 127, 3),
        (39, 40, 127, 127, 127, 127, 127, 2),
        (37, 43, 44, 127, 127, 127, 127, 0),
        (38, 41, 45, 49, 127, 127, 127, 1),
        (68, 42, 46, 51, 53, 56, 61, 35),
        (40, 127, 47, 50, 52, 59, 60, 34),
        (43, 44, 127, 48, 55, 57, 62, 36),
        (41, 45, 49, 127, 54, 58, 63, 32),
        (42, 74, 51, 53, 56, 61, 1, 38),
        (72, 47, 50, 52, 59, 60, 0, 33),
        (44, 46, 48, 55, 57, 62, 3, 43),
        (45, 49, 127, 54, 58, 63, 2, 40),
        (74, 51, 53, 56, 61, 1, 35, 37),
        (47, 50, 52, 59, 60, 0, 34, 92),
        (46, 48, 55, 57, 62, 3, 43, 44),
        (76, 81, 54, 58, 63, 2, 40, 42),
        (49, 83, 56, 84, 88, 35, 32, 39),
        (77, 82, 59, 87, 89, 45, 37, 41),
        (78, 80, 127, 40, 90, 43, 36, 46),
        (79, 52, 86, 63, 92, 95, 33, 47),
        (81, 85, 84, 127, 94, 40, 94, 127),
        (83, 127, 91, 127, 91, 93, 44, 127),
        (127, 127, 127, 127, 127, 37, 39, 127),
        (127, 127, 127, 127, 127, 127, 127, 127),
        (127, 127, 127, 127, 127, 127, 127, 127),
    ),
    (
        (33, 127, 127, 127, 127, 127, 127, 127),
        (35, 36, 127, 127, 127, 127, 127, 127),
        (32, 39, 40, 127, 127, 127, 127, 127),
        (34, 37, 43, 44, 127, 127, 127, 127),
        (65, 38, 41, 45, 49, 127, 127, 127),
        (67, 68, 42, 46, 51, 53, 56, 61),
        (64, 71, 72, 47, 50, 52, 59, 60),
        (66, 69, 75, 43, 48, 55, 57, 62),
        (127, 70, 73, 42, 46, 54, 58, 63),
        (127, 127, 74, 77, 47, 50, 52, 57),
        (71, 72, 38, 79, 45, 48, 55, 58),
        (69, 75, 76, 78, 44, 51, 54, 59),
        (70, 73, 77, 81, 42, 49, 53, 56),
        (93, 127, 78, 83, 85, 47, 50, 52),
        (92, 127, 79, 82, 84, 88, 48, 55),
        (75, 76, 32, 80, 87, 89, 51, 54),
        (73, 77, 81, 76, 86, 90, 49, 53),
        (89, 93, 83, 38, 40, 91, 47, 94),
        (90, 79, 82, 37, 38, 46, 45, 48),
        (91, 78, 80, 32, 41, 92, 93, 51),
        (88, 94, 127, 86, 33, 94, 95, 49),
        (84, 95, 85, 85, 93, 44, 46, 95),
        (87, 90, 92, 91, 43, 33, 89, 45),
        (86, 91, 94, 88, 83, 39, 90, 93),
        (85, 88, 95, 89, 80, 87, 88, 127),
        (82, 92, 87, 90, 81, 86, 92, 127),
        (80, 127, 88, 127, 95, 32, 41, 127),
        (127, 86, 127, 127, 127, 36, 127, 127),
        (127, 127, 127, 95, 127, 127, 127, 127),
        (127, 127, 127, 127, 127, 127, 127, 127),
    ),
)
STARTS = (0, 1, 2, 3, 4, 5, 5, 5)
NONE = 127
PARTS = 4
LEAD = 4
ROW = 8 * PARTS
PER_WORD = 4
BITS = 7
TOWARDS = (1, -1, 0)


def own_slots(link, leaving):
    table = ARRIVALS[link]
    rows = []
    for slot in range(len(table)):
        row = []
        for z in range(8):
            t, at = slot + STARTS[z], (z + TOWARDS[link]) % 8 if leaving else z
            v = table[t][at] if t < len(table) else NONE
            row.append(v - ROW if leaving and link == 2 and v != NONE else v)
        rows.append(row)
    while all(v == NONE for v in rows[-1]):
        rows.pop()
    return rows


COMING = [own_slots(link, False) for link in range(3)]
GOING = [own_slots(link, True) for link in range(3)]
SLOTS = max(len(table) for table in COMING)
SENDS = max(len(table) for table in GOING)
PAIRS = (SLOTS - 1) // 2


def first_slot(link, z):
    return min(t for t, row in enumerate(GOING[link]) if row[z] != NONE)


def packed_words(table, z):
    words = []
    table = table + [[NONE] * 8] * (-len(table) % PER_WORD)
    for first in range(0, len(table), PER_WORD):
        word = jnp.int32(0)
        for k in range(8):
            const = 0
            for i, row in enumerate(table[first : first + PER_WORD]):
                const += row[k] << (BITS * i)
            word = jnp.where(z == k, jnp.int32(const), word)
        words.append(word)
    return words


def look_up(words, slot):
    word = jnp.where(slot < len(words) * PER_WORD, words[-1], -1)
    for i in range(len(words) - 2, -1, -1):
        word = jnp.where(slot < (i + 1) * PER_WORD, words[i], word)
    return lax.shift_right_logical(word, BITS * lax.rem(slot, PER_WORD)) & (2**BITS - 1)


def kernel(
    q_ref, k_ref, v_ref, len_ref, out_ref, log_ref,
    buf, q_near, q_far, q_all, acc, peak, bounds, lengths, staged, log_out, log_in,
    send_sem, recv_sem, ready, local_sem, trade_send, trade_recv, out_send, out_recv, log_sem,
):
    ctx, x = lax.axis_index("ctx"), lax.axis_index("tp")
    core, z, y = lax.rem(ctx, 2), lax.rem(ctx // 2, 8), ctx // 16

    def device(dy=0, dz=0, dcore=0, dx=0):
        yy, zz = lax.rem(y + dy + 8, 8), lax.rem(z + dz + 8, 8)
        return ((yy * 8 + zz) * 2 + lax.rem(core + dcore, 2), lax.rem(x + dx, 4))

    link_to = (device(dz=1), device(dz=-1), device(dy=1))

    barrier = pltpu.get_barrier_semaphore()

    def signal(semaphore, to):
        pl.semaphore_signal(semaphore, inc=1, device_id=to, device_id_type=MESH)

    signal(barrier, device(dy=-1))
    for half in range(2):
        for dx in range(4):
            if half + dx:
                signal(barrier, device(dcore=half, dx=dx))

    @pl.when(z < 7)
    def _():
        signal(barrier, device(dz=1))

    @pl.when(z == 0)
    def _():
        signal(barrier, device(dz=-1))

    own = z * PARTS
    width = GROUP * HEAD_DIM
    mine = pl.ds(pl.multiple_of(core * HEAD_DIM, HEAD_DIM), HEAD_DIM)
    theirs = pl.ds(pl.multiple_of((1 - core) * HEAD_DIM, HEAD_DIM), HEAD_DIM)
    mine_q = pl.ds(pl.multiple_of(core * width, HEAD_DIM), width)
    theirs_q = pl.ds(pl.multiple_of((1 - core) * width, HEAD_DIM), width)
    local = []

    def bring(src, dst):
        local.append(pltpu.make_async_copy(src, dst, local_sem.at[len(local)]))

    def part(ref, i, columns):
        return ref.at[pl.ds(i * CHUNK, CHUNK), columns]

    for i in range(2):
        bring(part(k_ref, i, mine), buf.at[own + i, pl.ds(0, CHUNK)])
        bring(part(v_ref, i, mine), buf.at[own + i, pl.ds(CHUNK, CHUNK)])
    bring(q_ref.at[:, mine_q], q_near)
    bring(len_ref, lengths)
    for copy in local:
        copy.start()

    rx = [packed_words(COMING[link], z) for link in range(3)]
    tx = [packed_words(GOING[link], z) for link in range(3)]
    first_up = jnp.int32(-1)
    for k in range(7):
        first_up = jnp.where(z == k, first_slot(0, k), first_up)

    other = device(dcore=1)

    def trade(i, src, dst):
        return pltpu.make_async_remote_copy(
            src_ref=src, dst_ref=dst, send_sem=trade_send.at[i], recv_sem=trade_recv.at[i],
            device_id=other, device_id_type=MESH,
        )

    trades = []
    for i in range(2):
        trades.append(trade(2 * i, part(k_ref, i, theirs), buf.at[own + 2 + i, pl.ds(0, CHUNK)]))
        trades.append(
            trade(2 * i + 1, part(v_ref, i, theirs), buf.at[own + 2 + i, pl.ds(CHUNK, CHUNK)])
        )
    trades.append(trade(4, q_ref.at[:, theirs_q], q_far))

    def move(link, slot, chunk):
        landing = chunk + ROW if link == 2 else chunk
        return pltpu.make_async_remote_copy(
            src_ref=buf.at[chunk], dst_ref=buf.at[landing],
            send_sem=send_sem.at[link, slot], recv_sem=recv_sem.at[landing],
            device_id=link_to[link], device_id_type=MESH,
        )

    def leaving(link, slot):
        chunk = look_up(tx[link], slot)
        there = (chunk != NONE) & (chunk // ROW <= y)
        return chunk, (there & (y < 7)) if link == 2 else there

    def send(slot):
        for link in (2, 1, 0):
            chunk, there = leaving(link, slot)
            if link == 1:

                @pl.when((z == 0) & (slot == first_slot(1, 0)))
                def _():
                    pl.semaphore_wait(ready.at[1], 1)

            if link == 0:

                @pl.when(slot == first_up)
                def _():
                    pl.semaphore_wait(ready.at[0], 1)

            @pl.when(there)
            def _(link=link, chunk=chunk):
                move(link, slot, chunk).start()

    pl.semaphore_wait(barrier, 8 + jnp.where(z > 0, 1, 0) + jnp.where(z == 7, 1, 0))

    @pl.when(z > 0)
    def _():
        signal(ready.at[0], device(dz=-1))

    @pl.when(z == 7)
    def _():
        signal(ready.at[1], device(dz=1))

    for t in trades[:4]:
        t.start()
    for copy in local[:4]:
        copy.wait()
    send(jnp.int32(0))
    trades[4].start()

    local[5].wait()
    lane = lax.broadcasted_iota(jnp.int32, (1, HEAD_DIM), 1)
    starts = jnp.zeros((1, HEAD_DIM), jnp.int32)
    ends = jnp.zeros((1, HEAD_DIM), jnp.int32)
    end = jnp.int32(0)
    for i in range(DOCS):
        starts = jnp.where(lane == i, end, starts)
        end = end + lengths[i]
        ends = jnp.where(lane == i, end, ends)
    bounds[0:1, :] = starts
    bounds[1:2, :] = ends

    def in_document(base, rows):
        pos = base + lax.broadcasted_iota(jnp.int32, (rows, HEAD_DIM), 0)
        return (pos >= bounds[0:1, :]) & (pos < bounds[1:2, :])

    q_base = [(ctx - core + lax.rem(core + half, 2)) * ROWS for half in range(2)]
    for half in range(2):
        one_hot = jnp.where(in_document(q_base[half], ROWS), 1.0, 0.0).astype(jnp.bfloat16)
        for g in range(GROUP):
            b = 2 * g + half
            q_all[b * ROWS : (b + 1) * ROWS, HEAD_DIM:] = one_hot
    local[4].wait()
    for t in trades[:4]:
        t.wait_recv()
    send(jnp.int32(1))
    trades[4].wait_recv()
    for half, q_half in enumerate((q_near, q_far)):
        for g in range(GROUP):
            b = 2 * g + half
            q_all[b * ROWS : (b + 1) * ROWS, :HEAD_DIM] = q_half[
                :, g * HEAD_DIM : (g + 1) * HEAD_DIM
            ]

    halves = (slice(0, HEAD_DIM), slice(HEAD_DIM, 2 * HEAD_DIM))

    def load(chunks):
        keys, values = [], []
        for chunk, base in chunks:
            apart = jnp.where(in_document(base, CHUNK), 0.0, -APART).astype(jnp.bfloat16)
            keys.append(jnp.concatenate([buf[chunk, :CHUNK, :], apart], axis=1))
            ones = jnp.ones((CHUNK, HEAD_DIM), jnp.bfloat16)
            values.append(jnp.concatenate([buf[chunk, CHUNK:, :], ones], axis=1))
        keys = [jnp.concatenate(keys[i : i + 2], axis=0) for i in range(0, len(keys), 2)]
        return keys, jnp.concatenate(values, axis=0)

    def attend(b, keys, values, bases=None):
        rows = slice(b * ROWS, (b + 1) * ROWS)
        q = q_all[rows, :]
        scores = []
        for k in keys:
            s = lax.dot_general(
                q, k, (((1,), (1,)), ((), ())), preferred_element_type=jnp.float32
            )
            scores += [s[:, i : i + CHUNK] for i in range(0, k.shape[0], CHUNK)]
        if bases is not None:
            q_pos = q_base[b % 2] + lax.broadcasted_iota(jnp.int32, (ROWS, CHUNK), 0)
            lane_pos = lax.broadcasted_iota(jnp.int32, (ROWS, CHUNK), 1)
            scores = [
                jnp.where(base + lane_pos <= q_pos, s, NEG) for s, base in zip(scores, bases)
            ]
        top = scores[0]
        for s in scores[1:]:
            top = jnp.maximum(top, s)
        top = jnp.max(top, axis=1, keepdims=True)
        if bases is None:
            before = peak[rows, :]
            top = jnp.maximum(before, top)
            factor = jnp.exp2((before - top) * TO_EXP2)
        else:
            top = jnp.broadcast_to(top, (ROWS, HEAD_DIM))
        weights = [jnp.exp2((s - top) * TO_EXP2).astype(jnp.bfloat16) for s in scores]
        update = jnp.dot(
            jnp.concatenate(weights, axis=1), values, preferred_element_type=jnp.float32
        )
        peak[rows, :] = top
        for h in halves:
            acc[rows, h] = update[:, h] if bases is not None else acc[rows, h] * factor + update[:, h]

    def base_of(chunk, there):
        back, s, part = chunk // ROW, lax.rem(chunk // PARTS, 8), lax.rem(chunk, PARTS)
        base = (((y - back) * 8 + s) * 2 + lax.rem(part // 2 + core, 2)) * ROWS
        return jnp.where(there, base + lax.rem(part, 2) * CHUNK, -ROWS)

    bases = [q_base[i // 2] + (i % 2) * CHUNK for i in range(PARTS)]
    keys, values = load([(own + i, base) for i, base in enumerate(bases)])
    for b in range(2 * GROUP):
        attend(b, keys, values, bases)
        if b % GROUP == 0:
            for slot in range(2 + b // GROUP, LEAD, 2):
                send(jnp.int32(slot))

    def arrived(slot):
        chunks, some = [], False
        for link in range(3):
            chunk = look_up(rx[link], slot)
            there = (chunk != NONE) & (chunk // ROW <= y)
            safe = jnp.where(there, chunk, own)

            @pl.when(there)
            def _(safe=safe):
                pltpu.make_async_remote_copy(
                    src_ref=buf.at[safe], dst_ref=buf.at[safe],
                    send_sem=send_sem.at[0, slot], recv_sem=recv_sem.at[safe],
                    device_id=other, device_id_type=MESH,
                ).wait_recv()

            chunks.append((safe, base_of(chunk, there)))
            some = there | some
        return chunks, some

    def step(pair, carry):
        chunks, some = arrived(2 * pair)
        send(2 * pair + LEAD)
        more, any_more = arrived(2 * pair + 1)
        some = some | any_more
        send(2 * pair + LEAD + 1)

        @pl.when(some)
        def _():
            keys, values = load(chunks + more)
            for b in range(2 * GROUP):
                attend(b, keys, values)

        return carry

    lax.fori_loop(0, PAIRS, step, 0)

    last = []
    for slot in range(2 * PAIRS, SLOTS):
        last += arrived(jnp.int32(slot))[0]
        send(jnp.int32(slot + LEAD))

    def send_rest(slot, carry):
        send(slot)
        return carry

    lax.fori_loop(SLOTS + LEAD, SENDS, send_rest, 0)

    share = ROWS // 4
    sends = []
    keys, values = load(last)
    for b in range(2 * GROUP):
        attend(b, keys, values)
        g, half = b // 2, b % 2
        rows = slice(b * ROWS, (b + 1) * ROWS)
        staged[rows, :] = (acc[rows, :HEAD_DIM] / acc[rows, HEAD_DIM:]).astype(jnp.bfloat16)
        spot = pl.ds(pl.multiple_of((2 * x + core) * width + g * HEAD_DIM, HEAD_DIM), HEAD_DIM)
        for dx in range(4):
            to = lax.rem(x + dx, 4)
            piece = pl.ds(pl.multiple_of(b * ROWS + to * share, share), share)
            if half + dx == 0:
                out_ref[:, spot] = staged[piece, :]
                continue
            copy = pltpu.make_async_remote_copy(
                src_ref=staged.at[piece], dst_ref=out_ref.at[:, spot],
                send_sem=out_send.at[b, dx], recv_sem=out_recv.at[b, dx],
                device_id=device(dcore=half, dx=dx), device_id_type=MESH,
            )
            copy.start()
            sends.append(copy)

    for b in (1, 3, 5, 0, 2, 4):
        rows = slice(b * ROWS, (b + 1) * ROWS)
        log = (peak[rows, :] * SCALE + jnp.log(acc[rows, HEAD_DIM:])).T
        log_out[b % 2, b // 2 : b // 2 + 1, :] = log[:1, :]
        if b == 5:
            log_copy = pltpu.make_async_remote_copy(
                src_ref=log_out.at[1], dst_ref=log_in,
                send_sem=log_sem.at[0], recv_sem=log_sem.at[1],
                device_id=other, device_id_type=MESH,
            )
            log_copy.start()

    for t in trades:
        t.wait_send()

    def drain(slot, carry):
        for link in range(3):
            chunk, there = leaving(link, slot)

            @pl.when(there)
            def _(link=link, chunk=chunk):
                move(link, slot, chunk).wait_send()

        return carry

    lax.fori_loop(0, SENDS, drain, 0)
    log_copy.wait()
    near, far = log_out[0, :GROUP, :], log_in[:GROUP, :]
    log_ref[:GROUP, :] = jnp.where(core == 0, near, far)
    log_ref[GROUP:, :] = jnp.where(core == 0, far, near)
    for copy in sends:
        copy.wait()


def on_device(queries, keys, values, doc_lengths):
    columns = 4 * queries.shape[1]
    dma = pltpu.SemaphoreType.DMA
    bf16, f32 = jnp.bfloat16, jnp.float32
    vmem = pl.BlockSpec(memory_space=pltpu.VMEM)
    return pl.pallas_call(
        kernel,
        out_shape=(
            jax.ShapeDtypeStruct((ROWS // 4, columns), bf16),
            jax.ShapeDtypeStruct((2 * GROUP, ROWS), f32),
        ),
        in_specs=[pl.BlockSpec(memory_space=pltpu.HBM)] * 4,
        out_specs=(vmem, vmem),
        scratch_shapes=[
            pltpu.VMEM((3 * ROW, 2 * CHUNK, HEAD_DIM), bf16),
            pltpu.VMEM((ROWS, GROUP * HEAD_DIM), bf16),
            pltpu.VMEM((ROWS, GROUP * HEAD_DIM), bf16),
            pltpu.VMEM((2 * GROUP * ROWS, 2 * HEAD_DIM), bf16),
            pltpu.VMEM((2 * GROUP * ROWS, 2 * HEAD_DIM), f32),
            pltpu.VMEM((2 * GROUP * ROWS, HEAD_DIM), f32),
            pltpu.VMEM((8, HEAD_DIM), jnp.int32),
            pltpu.SMEM((DOCS,), jnp.int32),
            pltpu.VMEM((2 * GROUP * ROWS, HEAD_DIM), bf16),
            pltpu.VMEM((2, 8, ROWS), f32),
            pltpu.VMEM((8, ROWS), f32),
            dma((3, SENDS)),
            dma((3 * ROW,)),
            pltpu.SemaphoreType.REGULAR((2,)),
            dma((6,)),
            dma((5,)),
            dma((5,)),
            dma((2 * GROUP, 4)),
            dma((2 * GROUP, 4)),
            dma((2,)),
        ],
        compiler_params=pltpu.CompilerParams(
            collective_id=0, has_side_effects=True, vmem_limit_bytes=int(63.9 * 2**20)
        ),
        cost_estimate=pl.CostEstimate(
            flops=8 * 10**9, bytes_accessed=2 * 10**6, transcendentals=14 * 10**6
        ),
    )(queries, keys, values, doc_lengths)


def solution(mesh):
    in_specs = (P("ctx", "tp"), P("ctx", "tp"), P("ctx", "tp"), P())
    out_specs = (P(("ctx", "tp"), None), P("tp", "ctx"))
    return jax.shard_map(
        on_device, mesh=mesh, in_specs=in_specs, out_specs=out_specs, check_vma=False
    )
```

time: 60.6 us -> 60.6 us (level)
  the two profiles are of different devices: /device:TPU:32 before, /device:TPU:25 now
where the time goes in v3:
time: 60.6 us; the launch traced here: 60.4 us
  Pallas kernels  57.4 us (95%)
  local copies, waits for them, and re-layouts  2.37 us (4%)
  between operations  0.65 us (1%)
    pallas_call x1, Pallas kernels, on_device(): pl.pallas_call(kernel, out_shape=(jax.ShapeDtypeStruct((ROWS // 4, column...  57.4 us
    unnamed x4, local copies, waits for them, and re-layouts  2.37 us

profile of v3, /device:TPU:25, one launch (start us, length us, event | category | flops | bytes accessed | tf_op | source)
XLA Modules:
  0.0 60.4 jit_solution(6002919851981834542)
XLA Ops:
  0.6 57.4 %shard_map.59 = (bf16[64,3072]{1,0:T(8,128)(2,1)}, f32[6,256]{1,0:T(8,128)}) custom-call(bf16[256,768]{1,0:T(8,128)(2,1)} %q_ref.1, bf16[256,256]{1,0:T(8,128)(2,1)} %k_ref.1, bf16[256,256]{1,0:T(8,128)(2,1)} %v_ref.1, s32[16]{0:T(128)} %len_ref.1), custom_call_target="tpu_custom_call" | custom-call | flops 8000000000 | bytes 2000000 | tf_op jit(solution)/shard_map/pallas_call | solution.py:503
  58.0 0.0 copy-start
  58.1 1.8 %copy.8 = bf16[64,3072]{1,0:T(8,128)(2,1)} copy(bf16[64,3072]{1,0:T(8,128)(2,1)} %get-tuple-element.4) | data formatting | bytes 786432
  59.8 0.0 copy-done
  59.8 0.6 copy.9
Async XLA Ops:
  58.0 1.8 %copy-start = (f32[6,256]{1,0:T(8,128)S(1)}, f32[6,256]{1,0:T(8,128)}, u32[]{:S(2)}) copy-start(f32[6,256]{1,0:T(8,128)} %get-tuple-element.5) | copy-start | bytes 18436
